TPU v7x, 512 devices: a whole 4x4x16 slice. The times are simulated.
512 devices in a mesh: seq: 128 (over z, x, core), mp: 4 (over y).
Axes of the slice: x: 4, y: 4, z: 16, core: 2. Of those that a mesh axis runs over, the one named last changes fastest.
Arguments:
- queries: bfloat16 [16384, 4096], P('seq', 'mp'), may hold values from -6 to 6
- keys: bfloat16 [16384, 4096], P('seq', 'mp'), may hold values from -6 to 6
- values: bfloat16 [16384, 4096], P('seq', 'mp'), may hold values from -6 to 6
- log_decay: float32 [16384, 32], P('seq', 'mp'), may hold values from -0.7 to 0, as said below
- norm_gain: float32 [4096], P('mp'), may hold values from 0.1 to 1.9
Outputs:
- attended: bfloat16 [16384, 4096], P(('seq', 'mp'))
Inputs may be any that keep to these rules, and one draw needn't show every extreme that they name: `log_decay`: each entry is the logarithm of a decay factor in (0, 1].
All inputs are finite; a program needn't handle non-finite values.
Results may differ from a plain program's by a relative error of at most 0.0056.
Values may be sent and summed in bfloat16 or wider, within the bound.
No kernel may reach another device: no remote copies, remote signals or barrier semaphores. Data moves between devices by JAX's collectives and lax.ppermute only.
A program may use at most 192 MiB of HBM per device.

v0:
```python
import jax
import jax.numpy as jnp
from jax import lax
from jax.sharding import PartitionSpec as P

HEAD_DIM = 128


def carried_in(part, axis, combine, identity):
    place = lax.axis_index(axis)
    gathered = jax.tree.map(lambda a: lax.all_gather(a, axis), part)
    state = jax.tree.map(lambda a, e: jnp.zeros_like(a) + jnp.asarray(e, a.dtype), part, identity)

    def one(lap, state):
        return combine(
            state, jax.tree.map(lambda a: lax.dynamic_index_in_dim(a, lap, 0, False), gathered)
        )

    return lax.fori_loop(0, place, one, state)


def combine(earlier, later):
    decay_e, state_e = earlier
    decay_l, state_l = later
    return (decay_e * decay_l, decay_l[:, None, None] * state_e + state_l)


def body(queries, keys, values, log_decay, norm_gain):
    tok_rows = queries.shape[0]
    heads_here = log_decay.shape[1]
    kh = keys.reshape(tok_rows, heads_here, HEAD_DIM)
    vh = values.reshape(tok_rows, heads_here, HEAD_DIM)
    cum = jnp.cumsum(log_decay, axis=0)
    last = cum[-1]
    scaled_keys = (kh * jnp.exp(last[None, :] - cum)[:, :, None]).astype(jnp.bfloat16)
    block_state = jnp.einsum("thd,the->hde", scaled_keys, vh, preferred_element_type=jnp.float32)
    block_decay = jnp.exp(last)
    identity = (jnp.ones_like(block_decay), jnp.zeros_like(block_state))
    prior_decay, prior_state = carried_in((block_decay, block_state), "seq", combine, identity)
    prior_rounded = prior_state.astype(jnp.bfloat16)
    rows = jnp.arange(tok_rows)
    causal = rows[:, None] >= rows[None, :]
    gains = norm_gain.reshape(heads_here, HEAD_DIM)

    def one_head(head):
        q_head = lax.dynamic_slice_in_dim(queries, head * HEAD_DIM, HEAD_DIM, 1)
        k_head = lax.dynamic_slice_in_dim(keys, head * HEAD_DIM, HEAD_DIM, 1)
        v_head = lax.dynamic_slice_in_dim(values, head * HEAD_DIM, HEAD_DIM, 1)
        cum_head = lax.dynamic_slice_in_dim(cum, head, 1, 1)[:, 0]
        state_head = lax.dynamic_index_in_dim(prior_rounded, head, 0, False)
        gain_head = lax.dynamic_index_in_dim(gains, head, 0, False)
        diff = cum_head[:, None] - cum_head[None, :]
        factor = jnp.where(causal, jnp.exp(jnp.minimum(diff, 0.0)), 0.0)
        scores = lax.dot_general(
            q_head, k_head, (((1,), (1,)), ((), ())), preferred_element_type=jnp.float32
        )
        weights = (scores * factor).astype(jnp.bfloat16)
        inner = jnp.dot(weights, v_head, preferred_element_type=jnp.float32)
        outer = jnp.dot(q_head, state_head, preferred_element_type=jnp.float32)
        mixed = inner + outer * jnp.exp(cum_head)[:, None]
        scale = lax.rsqrt(jnp.mean(mixed * mixed, axis=-1, keepdims=True) + 1e-05)
        return (mixed * scale * gain_head[None]).astype(jnp.bfloat16)

    per_head = lax.map(one_head, jnp.arange(heads_here, dtype=jnp.int32))
    normed = jnp.transpose(per_head, (1, 0, 2)).reshape(tok_rows, heads_here * HEAD_DIM)
    return lax.all_to_all(normed, "mp", split_axis=0, concat_axis=1, tiled=True)


def solution(mesh):
    in_specs = (P("seq", "mp"), P("seq", "mp"), P("seq", "mp"), P("seq", "mp"), P("mp"))
    out_specs = P(("seq", "mp"), None)
    return jax.shard_map(body, mesh=mesh, in_specs=in_specs, out_specs=out_specs, check_vma=False)
```

profile of v0, /device:TPU:487, one launch (start us, length us, event | category | flops | bytes accessed | tf_op | source)
XLA Modules:
  0.0 527.4 jit_solution(16934100050708300561)
XLA Ops:
  8.7 2.0 fusion.28
  10.7 71.9 %all-gather.1 = f32[128,1,8]{2,1,0:T(1,128)S(1)} all-gather(f32[1,1,8]{2,1,0:T(1,128)S(1)} %get-tuple-element.192), channel_id=1, replica_groups=mesh['seq'=128,'mp'=4] {'seq'}, dimensions={0}, use_global_device_ids=true | all-gather | bytes 4128 | tf_op jit(solution)/shard_map/all_gather | solution.py:11
  82.6 219.9 %all-gather.4.cloned.1.call-done = f32[1024,128,128]{2,1,0:T(8,128)} async-done(((f32[8,128,128]{2,1,0:T(8,128)}), f32[1024,128,128]{2,1,0:T(8,128)}) %all-gather.4.cloned.1.call-update) | async-done | bytes 67108880 | tf_op jit(solution)/shard_map/all_gather | solution.py:11
  302.5 157.2 %while.23 = (s32[]{:T(128)}, f32[8,128,128]{2,1,0:T(8,128)S(1)}, s32[]{:T(128)}, f32[128,8]{1,0:T(8,128)S(1)}, f32[128,8,128,128]{3,2,1,0:T(8,128)}, /*index=5*/s32[]{:T(128)}, s32[]{:T(128)}, s32[]{:T(128)}) while((s32[]{:T(128)}, f32[8,128,128]{2,1,0:T(8,128)S(1)}, s32[]{:T(128)}, f32[128,8]{1,0:T(8,128)S(1)}, ...), condition=%wide.region_2.3_spmd, body=%wide.region_1.2_spmd.sunk | while | flops 262149 | bytes 1573087 | solution.py:19
  302.6 1.2 bitcast_add_fusion.2
  303.8 1.2 bitcast_add_fusion.2
  305.0 1.2 bitcast_add_fusion.2
  306.3 1.2 bitcast_add_fusion.2
  307.5 1.2 bitcast_add_fusion.2
  308.8 1.2 bitcast_add_fusion.2
  310.0 1.2 bitcast_add_fusion.2
  311.2 1.2 bitcast_add_fusion.2
  312.5 1.2 bitcast_add_fusion.2
  313.7 1.2 bitcast_add_fusion.2
  314.9 1.2 bitcast_add_fusion.2
  316.2 1.2 bitcast_add_fusion.2
  317.4 1.2 bitcast_add_fusion.2
  318.7 1.2 bitcast_add_fusion.2
  319.9 1.2 bitcast_add_fusion.2
  321.1 1.2 bitcast_add_fusion.2
  322.4 1.2 bitcast_add_fusion.2
  323.6 1.2 bitcast_add_fusion.2
  324.9 1.2 bitcast_add_fusion.2
  326.1 1.2 bitcast_add_fusion.2
  327.3 1.2 bitcast_add_fusion.2
  328.6 1.2 bitcast_add_fusion.2
  329.8 1.2 bitcast_add_fusion.2
  331.0 1.2 bitcast_add_fusion.2
  332.3 1.2 bitcast_add_fusion.2
  333.5 1.2 bitcast_add_fusion.2
  336.0 1.2 bitcast_add_fusion.2
  340.9 1.2 bitcast_add_fusion.2
  345.9 1.2 bitcast_add_fusion.2
  349.6 1.2 bitcast_add_fusion.2
  350.8 1.2 bitcast_add_fusion.2
  354.6 1.2 bitcast_add_fusion.2
  359.5 1.2 bitcast_add_fusion.2
  364.5 1.2 bitcast_add_fusion.2
  369.4 1.2 bitcast_add_fusion.2
  373.1 1.2 bitcast_add_fusion.2
  374.4 1.2 bitcast_add_fusion.2
  378.1 1.2 bitcast_add_fusion.2
  383.0 1.2 bitcast_add_fusion.2
  388.0 1.2 bitcast_add_fusion.2
  392.9 1.2 bitcast_add_fusion.2
  396.7 1.2 bitcast_add_fusion.2
  397.9 1.2 bitcast_add_fusion.2
  401.6 1.2 bitcast_add_fusion.2
  406.6 1.2 bitcast_add_fusion.2
  411.5 1.2 bitcast_add_fusion.2
  416.5 1.2 bitcast_add_fusion.2
  420.2 1.2 bitcast_add_fusion.2
  421.4 1.2 bitcast_add_fusion.2
  425.1 1.2 bitcast_add_fusion.2
  430.1 1.2 bitcast_add_fusion.2
  435.0 1.2 bitcast_add_fusion.2
  440.0 1.2 bitcast_add_fusion.2
  443.7 1.2 bitcast_add_fusion.2
  444.9 1.2 bitcast_add_fusion.2
  448.6 1.2 bitcast_add_fusion.2
  453.6 1.2 bitcast_add_fusion.2
  458.5 1.2 bitcast_add_fusion.2
  459.8 49.2 %while.24 = (s32[]{:T(128)}, bf16[8,128,128]{1,2,0:T(8,128)(2,1)S(1)}, s32[8]{0:T(128)S(1)}, bf16[128,1024]{1,0:T(8,128)(2,1)}, bf16[128,1024]{1,0:T(8,128)(2,1)...) while((s32[]{:T(128)}, ...), condition=%wide.region_5.6_spmd.clone, body=%wide.region_3.5_spmd.clone.sunk | while | flops 12796041 | bytes 467189 | solution.py:64
  509.3 10.5 %all_to_all.19 = bf16[4,32,1024]{2,1,0:T(8,128)(2,1)S(1)} all-to-all(bf16[4,32,1024]{2,1,0:T(8,128)(2,1)S(1)} %all_to_all.14), channel_id=1, replica_groups=mesh['seq'=128,'mp'=4] {'mp'}, dimensions={0} | all-to-all | bytes 524288 | tf_op jit(solution)/shard_map/all_to_all | solution.py:66
  (268 shorter events, 115.5 us)
Async XLA Ops:
  6.5 296.0 %all-gather.4.cloned.1.call-start = ((), (), s32[]{:S(2)}) async-start(), calls=%async_computation.1 | async-start | bytes 67633152 | tf_op jit(solution)/shard_map/all_gather | solution.py:11
Sparse Core Ops, SparseCore 0:
  10.8 291.6 all-gather.3
where the time goes:
time: 535 us; the launch traced here: 527 us
  waiting for transfers between devices  220 us (41%)
  other arithmetic  152 us (28%)
  blocking collectives  82.4 us (15%)
  loops' own time  25.1 us (5%)
  matrix products  18.8 us (4%)
  local copies, waits for them, and re-layouts  15.5 us (3%)
  between operations  13.5 us (3%)
    all_gather x1, waiting for transfers between devices, carried_in(): gathered = jax.tree.map(lambda a: lax.all_gather(a, axis), part)  220 us
    add x127, other arithmetic, combine(): return (decay_e * decay_l, decay_l[:, None, None] * state_e + state_l)  151 us
    all_gather x1, blocking collectives, carried_in(): gathered = jax.tree.map(lambda a: lax.all_gather(a, axis), part)  71.9 us
    another operation x1, loops' own time, body(): per_head = lax.map(one_head, jnp.arange(heads_here, dtype=jnp.int32))  20.6 us
  transfers between devices with their start and end apart: 1, of which 1 were waited for; matrix products, arithmetic and copies ran while one was open for 0% of the time, Pallas kernels for 0%

commit v1 on v0

v1 whole, which is shorter than its diff:
```python
import functools

import jax
import jax.numpy as jnp
from jax import lax
from jax.experimental import pallas as pl
from jax.experimental.pallas import tpu as pltpu
from jax.sharding import Mesh, PartitionSpec as P

HEAD_DIM = 128
F32 = jnp.float32
B16 = jnp.bfloat16
EXTRA = 16
GROUP = ("zl", "x", "c")


def pieces3(a):
    hi = a.astype(B16)
    rest = a - hi.astype(F32)
    mid = rest.astype(B16)
    return hi, mid, (rest - mid.astype(F32)).astype(B16)


def triangle(n):
    r = lax.broadcasted_iota(jnp.int32, (n, n), 0)
    c = lax.broadcasted_iota(jnp.int32, (n, n), 1)
    return r >= c


def cumulative(g):
    low = triangle(g.shape[0]).astype(F32).astype(B16)
    hi, mid, lo = (jnp.dot(low, p, preferred_element_type=F32) for p in pieces3(g))
    return hi + (mid + lo)


def decay_rows(d):
    d = jnp.broadcast_to(d, (EXTRA, HEAD_DIM))
    hi, mid, lo = (p.astype(F32) for p in pieces3(d))
    row = lax.broadcasted_iota(jnp.int32, d.shape, 0)
    out = jnp.where(row == 0, hi, jnp.where(row == 1, mid, jnp.where(row == 2, lo, 0.0)))
    return out.astype(B16)


def read_decay(rows):
    r = rows.astype(F32)
    return r[0:1] + (r[1:2] + r[2:3])


def states_kernel(k_ref, v_ref, g_ref, o_ref):
    heads = g_ref.shape[1]
    half = o_ref.shape[1] - EXTRA
    cuts = HEAD_DIM // half
    cum = cumulative(g_ref[...])
    last = cum[-1:]
    to_end = jnp.exp(last - cum)
    whole = jnp.exp(last)
    for h in range(heads):
        cols = slice(h * HEAD_DIM, (h + 1) * HEAD_DIM)
        scaled = (k_ref[:, cols].astype(F32) * to_end[:, h : h + 1]).astype(B16)
        state = lax.dot_general(
            scaled, v_ref[:, cols], (((0,), (0,)), ((), ())), preferred_element_type=F32
        ).astype(B16)
        rows = decay_rows(whole[:, h : h + 1])
        for i in range(cuts):
            o_ref[h * cuts + i, :half] = state[i * half : (i + 1) * half]
            o_ref[h * cuts + i, half:] = rows


def total_kernel(x_ref, o_ref):
    n, rows, _ = x_ref.shape
    half = rows - EXTRA
    state = x_ref[0, :half].astype(F32)
    decay = read_decay(x_ref[0, half:])
    for b in range(1, n):
        d = read_decay(x_ref[b, half:])
        state = d * state + x_ref[b, :half].astype(F32)
        decay = decay * d
    state = state.astype(B16)
    tail = decay_rows(decay)
    for j in range(o_ref.shape[0]):
        o_ref[j, :half] = state
        o_ref[j, half:] = tail


def prior_kernel(place_ref, z_ref, x_ref, o_ref):
    place = place_ref[0]
    n, half, _ = o_ref.shape
    state = jnp.zeros((half, HEAD_DIM), F32)
    for j in range(z_ref.shape[0] - 1):
        later = read_decay(z_ref[j, half:]) * state + z_ref[j, :half].astype(F32)
        state = jnp.where(j < place, later, state)
    for b in range(n):
        o_ref[b] = state.astype(B16)
        if b < n - 1:
            state = read_decay(x_ref[b, half:]) * state + x_ref[b, :half].astype(F32)


def inner_kernel(q_ref, k_ref, v_ref, g_ref, gt_ref, o_ref):
    heads = g_ref.shape[1]
    tok = g_ref.shape[0]
    cum = cumulative(g_ref[...])
    up = triangle(tok).astype(F32).astype(B16)
    cum_t = sum(
        lax.dot_general(p, up, (((1,), (1,)), ((), ())), preferred_element_type=F32)
        for p in pieces3(gt_ref[...])[::-1]
    )
    causal = triangle(tok)
    for h in range(heads):
        cols = slice(h * HEAD_DIM, (h + 1) * HEAD_DIM)
        scores = lax.dot_general(
            q_ref[:, cols], k_ref[:, cols], (((1,), (1,)), ((), ())), preferred_element_type=F32
        )
        diff = cum[:, h : h + 1] - cum_t[h : h + 1, :]
        factor = jnp.where(causal, jnp.exp(jnp.minimum(diff, 0.0)), 0.0)
        weights = (scores * factor).astype(B16)
        o_ref[:, cols] = jnp.dot(weights, v_ref[:, cols], preferred_element_type=F32)


def output_kernel(q_ref, s_ref, i_ref, g_ref, gain_ref, o_ref):
    heads = g_ref.shape[1]
    grown = jnp.exp(cumulative(g_ref[...]))
    for h in range(heads):
        cols = slice(h * HEAD_DIM, (h + 1) * HEAD_DIM)
        outer = jnp.dot(q_ref[:, cols], s_ref[h], preferred_element_type=F32)
        mixed = i_ref[:, cols] + outer * grown[:, h : h + 1]
        mean = jnp.mean(mixed * mixed, axis=-1, keepdims=True)
        o_ref[:, cols] = (mixed * lax.rsqrt(mean + 1e-05) * gain_ref[:, cols]).astype(B16)


def local(kernel, shape, dtype, *args, flops=0, smem_first=False):
    specs = [pl.BlockSpec(memory_space=pltpu.VMEM)] * len(args)
    if smem_first:
        specs[0] = pl.BlockSpec(memory_space=pltpu.SMEM)
    moved = sum(a.size * a.dtype.itemsize for a in args)
    return pl.pallas_call(
        kernel,
        out_shape=jax.ShapeDtypeStruct(shape, dtype),
        in_specs=specs,
        out_specs=pl.BlockSpec(memory_space=pltpu.VMEM),
        compiler_params=pltpu.CompilerParams(vmem_limit_bytes=32 * 2**20),
        cost_estimate=pl.CostEstimate(flops=flops, bytes_accessed=moved, transcendentals=0),
    )(*args)


def body(groups, members, queries, keys, values, log_decay, norm_gain):
    tok, width = queries.shape
    heads = log_decay.shape[1]
    half = heads * HEAD_DIM // members
    mac = 2 * heads * tok * HEAD_DIM * HEAD_DIM
    own = local(states_kernel, (members, half + EXTRA, HEAD_DIM), B16, keys, values, log_decay, flops=mac)
    blocks = lax.all_to_all(own, GROUP, 0, 0, tiled=True)
    total = local(total_kernel, (groups, half + EXTRA, HEAD_DIM), B16, blocks)
    totals = lax.all_to_all(total, "zh", 0, 0, tiled=True)
    place = lax.axis_index("zh").astype(jnp.int32).reshape(1)
    prior = local(prior_kernel, (members, half, HEAD_DIM), B16, place, totals, blocks, smem_first=True)
    state = lax.all_to_all(prior, GROUP, 0, 0, tiled=True).reshape(heads, HEAD_DIM, HEAD_DIM)
    inner = local(
        inner_kernel, (tok, width), F32, queries, keys, values, log_decay, log_decay.T, flops=2 * mac
    )
    normed = local(
        output_kernel,
        (tok, width),
        B16,
        queries,
        state,
        inner,
        log_decay,
        norm_gain.reshape(1, width),
        flops=mac,
    )
    return lax.all_to_all(normed, "y", 0, 1, tiled=True)


def solution(mesh):
    seq, mp = mesh.devices.shape
    fine = Mesh(mesh.devices.reshape(seq // 16, 2, 4, 2, mp), ("zh", "zl", "x", "c", "y"))
    tokens = ("zh", "zl", "x", "c")
    in_specs = (P(tokens, "y"),) * 4 + (P("y"),)
    return jax.shard_map(
        functools.partial(body, seq // 16, 16),
        mesh=fine,
        in_specs=in_specs,
        out_specs=P((*tokens, "y"), None),
        check_vma=False,
    )
```

time: 535 us -> 74.2 us (0.14)
  the two profiles are of different devices: /device:TPU:487 before, /device:TPU:6 now
where the time goes in v1:
time: 74.2 us; the launch traced here: 73.3 us
  blocking collectives  26.3 us (35%)
  waiting for transfers between devices  21.8 us (29%)
  starting transfers between devices  17.2 us (23%)
  Pallas kernels  4.53 us (6%)
  local copies, waits for them, and re-layouts  3.42 us (5%)
    all_to_all x1, waiting for transfers between devices, body(): totals = lax.all_to_all(total, 'zh', 0, 0, tiled=True)  17.4 us
    all_to_all x1, blocking collectives, body(): blocks = lax.all_to_all(own, GROUP, 0, 0, tiled=True)  14.9 us
    all_to_all x1, starting transfers between devices, body(): totals = lax.all_to_all(total, 'zh', 0, 0, tiled=True)  11.8 us
    all_to_all x1, blocking collectives, body(): return lax.all_to_all(normed, 'y', 0, 1, tiled=True)  11.4 us
    all_to_all x1, starting transfers between devices, body(): lax.all_to_all(prior, GROUP, 0, 0, tiled=True)  5.39 us
    pallas_call x5, Pallas kernels, local(): pl.pallas_call(kernel, out_shape=jax.ShapeDtypeStruct(shape, dtype), in_s...  4.53 us
    all_to_all x1, waiting for transfers between devices, body(): lax.all_to_all(prior, GROUP, 0, 0, tiled=True)  4.4 us
    unnamed x15, local copies, waits for them, and re-layouts  2.7 us
  transfers between devices with their start and end apart: 2, of which 2 were waited for; matrix products, arithmetic and copies ran while one was open for 0% of the time, Pallas kernels for 2%

profile of v1, /device:TPU:6, one launch (start us, length us, event | category | flops | bytes accessed | tf_op | source)
XLA Modules:
  0.0 73.3 jit_solution(8581505189145655946)
XLA Ops:
  0.0 0.8 %copy.6.g_ref = f32[128,8]{1,0:T(8,128)S(1)} copy(f32[128,8]{0,1:T(8,128)} %param.8) | data formatting | bytes 8192 | tf_op args[3]
  0.8 0.0 copy-start
  0.8 0.9 %copy-done = bf16[128,1024]{1,0:T(8,128)(2,1)S(1)} copy-done((bf16[128,1024]{1,0:T(8,128)(2,1)S(1)}, bf16[128,1024]{1,0:T(8,128)(2,1)}, u32[]{:S(2)}) %copy-start) | copy-done | bytes 262168
  1.7 0.0 copy-start.2
  1.7 0.9 %copy-done.2 = bf16[128,1024]{1,0:T(8,128)(2,1)S(1)} copy-done((bf16[128,1024]{1,0:T(8,128)(2,1)S(1)}, bf16[128,1024]{1,0:T(8,128)(2,1)}, u32[]{:S(2)}) %copy-start.2) | copy-done | bytes 262168
  2.7 0.7 shard_map.55
  3.3 14.9 %all_to_all.34.x_ref = bf16[16,80,128]{2,1,0:T(8,128)(2,1)S(1)} all-to-all(bf16[16,80,128]{2,1,0:T(8,128)(2,1)S(1)} %shard_map.55), channel_id=1, replica_groups=mesh['zh'=8,'zl'=2,'x'=4,'c'=2,'y'=4] {'zl','x','c'}, dimensions={0} | all-to-all | bytes 655360 | tf_op jit(solution)/shard_map/all_to_all | solution.py:151
  18.3 0.7 %shard_map.56 = bf16[8,80,128]{2,1,0:T(8,128)(2,1)} custom-call(bf16[16,80,128]{2,1,0:T(8,128)(2,1)S(1)} %all_to_all.34.x_ref), custom_call_target="tpu_custom_call" | custom-call | bytes 327680 | tf_op jit(solution)/shard_map/pallas_call | solution.py:135
  19.0 11.8 %all-to-all-start.1 = ((bf16[8,80,128]{2,1,0:T(8,128)(2,1)}), bf16[8,80,128]{2,1,0:T(8,128)(2,1)S(1)}, u32[]{:S(2)}, u32[]{:S(2)}) async-start(bf16[8,80,128]{2,1,0:T(8,128)(2,1)} %shard_map.56), calls=%async_computation.1 | async-start | bytes 327680 | tf_op jit(solution)/shard_map/all_to_all | solution.py:153
  30.8 17.4 %all-to-all-done.1.z_ref = bf16[8,80,128]{2,1,0:T(8,128)(2,1)S(1)} async-done(((bf16[8,80,128]{2,1,0:T(8,128)(2,1)}), bf16[8,80,128]{2,1,0:T(8,128)(2,1)S(1)}, u32[]{:S(2)}, u32[]{:S(2)}) %all-to-all-start.1) | async-done | bytes 163872 | tf_op jit(solution)/shard_map/all_to_all | solution.py:153
  48.2 0.0 copy-start.4
  48.2 0.0 copy-start.5
  48.2 0.8 %shard_map.57 = bf16[16,64,128]{2,1,0:T(8,128)(2,1)} custom-call(s32[1]{0:T(128)} %bitcast.place_ref, bf16[8,80,128]{2,1,0:T(8,128)(2,1)S(1)} %all-to-all-done.1.z_ref, bf16[16,80,128]{2,1,0:T(8,128)(2,1)S(1)} %all_to_all.34.x_ref), custom_call_target="tpu_custom_call" | custom-call | bytes 491524 | tf_op jit(solution)/shard_map/pallas_call | solution.py:135
  49.0 0.0 copy-start.1
  49.0 0.0 copy-start.3
  49.0 5.4 %all-to-all-start.2 = ((bf16[16,64,128]{2,1,0:T(8,128)(2,1)}), bf16[16,64,128]{2,1,0:T(8,128)(2,1)S(1)}, u32[]{:S(2)}, u32[]{:S(2)}) async-start(bf16[16,64,128]{2,1,0:T(8,128)(2,1)} %shard_map.57), calls=%async_computation.2 | async-start | bytes 524288 | tf_op jit(solution)/shard_map/all_to_all | solution.py:156
  54.4 0.0 copy-done.4
  54.4 0.0 copy-done.5
  54.4 0.0 copy-done.1
  54.4 0.0 copy-done.3
  54.4 0.0 copy-start.6
  54.5 1.5 %shard_map.58.i_ref = f32[128,1024]{1,0:T(8,128)S(1)} custom-call(bf16[128,1024]{1,0:T(8,128)(2,1)S(1)} %copy-done.4, bf16[128,1024]{1,0:T(8,128)(2,1)S(1)} %copy-done.1, bf16[128,1024]{1,0:T(8,128)(2,1)S(1)} %copy-done.3, f32[128,8]{1,0:T(8,128)S(1)} %copy.6.g_ref, f32[8,128]{1,0:T(8,128)S(1)} %bitcast.10), custom_call_target="tpu_custom_call" | custom-call | flops 67108864 | bytes 794624 | tf_op jit(solution)/shard_map/pallas_call | solution.py:135
  55.9 4.4 %all-to-all-done.2 = bf16[16,64,128]{2,1,0:T(8,128)(2,1)S(1)} async-done(((bf16[16,64,128]{2,1,0:T(8,128)(2,1)}), bf16[16,64,128]{2,1,0:T(8,128)(2,1)S(1)}, u32[]{:S(2)}, u32[]{:S(2)}) %all-to-all-start.2) | async-done | bytes 262176 | tf_op jit(solution)/shard_map/all_to_all | solution.py:156
  60.3 0.0 copy-done.6
  60.3 0.9 %shard_map.59 = bf16[128,1024]{1,0:T(8,128)(2,1)S(1)} custom-call(bf16[128,1024]{1,0:T(8,128)(2,1)S(1)} %copy-done.4, bf16[8,128,128]{2,1,0:T(8,128)(2,1)S(1)} %bitcast.8, f32[128,1024]{1,0:T(8,128)S(1)} %shard_map.58.i_ref, f32[128,8]{1,0:T(8,128)S(1)} %copy.6.g_ref, f32[1,1024]{1,0:T(1,128)S(1)} %bitcast.11), custom_call_target="tpu_custom_call" | custom-call | flops 33554432 | bytes 1056768 | tf_op jit(solution)/shard_map/pallas_call | solution.py:135
  61.2 11.4 %all_to_all.35 = bf16[4,32,1024]{2,1,0:T(8,128)(2,1)S(1)} all-to-all(bf16[4,32,1024]{2,1,0:T(8,128)(2,1)S(1)} %bitcast.9), channel_id=1, replica_groups=mesh['zh'=8,'zl'=2,'x'=4,'c'=2,'y'=4] {'y'}, dimensions={0} | all-to-all | bytes 524288 | tf_op jit(solution)/shard_map/all_to_all | solution.py:171
  72.6 0.7 copy.10
Async XLA Ops:
  0.8 0.9 %copy-start = (bf16[128,1024]{1,0:T(8,128)(2,1)S(1)}, bf16[128,1024]{1,0:T(8,128)(2,1)}, u32[]{:S(2)}) copy-start(bf16[128,1024]{1,0:T(8,128)(2,1)} %k_ref.3) | copy-start | bytes 786436
  1.7 0.9 %copy-start.2 = (bf16[128,1024]{1,0:T(8,128)(2,1)S(1)}, bf16[128,1024]{1,0:T(8,128)(2,1)}, u32[]{:S(2)}) copy-start(bf16[128,1024]{1,0:T(8,128)(2,1)} %v_ref.3) | copy-start | bytes 786436
  19.0 29.2 %all-to-all-start.1 = ((bf16[8,80,128]{2,1,0:T(8,128)(2,1)}), bf16[8,80,128]{2,1,0:T(8,128)(2,1)S(1)}, u32[]{:S(2)}, u32[]{:S(2)}) async-start(bf16[8,80,128]{2,1,0:T(8,128)(2,1)} %shard_map.56), calls=%async_computation.1 | async-start | bytes 327680 | tf_op jit(solution)/shard_map/all_to_all | solution.py:153
  48.2 6.2 %copy-start.4 = (bf16[128,1024]{1,0:T(8,128)(2,1)S(1)}, bf16[128,1024]{1,0:T(8,128)(2,1)}, u32[]{:S(2)}) copy-start(bf16[128,1024]{1,0:T(8,128)(2,1)} %q_ref.3) | copy-start | bytes 786436
  48.2 6.2 %copy-start.5 = (f32[128,8]{0,1:T(8,128)S(1)}, f32[128,8]{0,1:T(8,128)}, u32[]{:S(2)}) copy-start(f32[128,8]{0,1:T(8,128)} %param.8) | copy-start | bytes 12292
  49.0 5.4 %copy-start.1 = (bf16[128,1024]{1,0:T(8,128)(2,1)S(1)}, bf16[128,1024]{1,0:T(8,128)(2,1)}, u32[]{:S(2)}) copy-start(bf16[128,1024]{1,0:T(8,128)(2,1)} %k_ref.3) | copy-start | bytes 786436
  49.0 5.4 %copy-start.3 = (bf16[128,1024]{1,0:T(8,128)(2,1)S(1)}, bf16[128,1024]{1,0:T(8,128)(2,1)}, u32[]{:S(2)}) copy-start(bf16[128,1024]{1,0:T(8,128)(2,1)} %v_ref.3) | copy-start | bytes 786436
  49.0 11.3 %all-to-all-start.2 = ((bf16[16,64,128]{2,1,0:T(8,128)(2,1)}), bf16[16,64,128]{2,1,0:T(8,128)(2,1)S(1)}, u32[]{:S(2)}, u32[]{:S(2)}) async-start(bf16[16,64,128]{2,1,0:T(8,128)(2,1)} %shard_map.57), calls=%async_computation.2 | async-start | bytes 524288 | tf_op jit(solution)/shard_map/all_to_all | solution.py:156
  54.4 5.9 %copy-start.6 = (f32[1024]{0:T(1024)S(1)}, f32[1024]{0:T(1024)}, u32[]{:S(2)}) copy-start(f32[1024]{0:T(1024)} %param.9) | copy-start | bytes 12292

commit v2 on v1

v2 whole, which is shorter than its diff:
```python
import functools

import jax
import jax.numpy as jnp
from jax import lax
from jax.experimental import pallas as pl
from jax.experimental.pallas import tpu as pltpu
from jax.sharding import Mesh, PartitionSpec as P

HEAD_DIM = 128
F32 = jnp.float32
B16 = jnp.bfloat16
EXTRA = 16


def pieces3(a):
    hi = a.astype(B16)
    rest = a - hi.astype(F32)
    mid = rest.astype(B16)
    return hi, mid, (rest - mid.astype(F32)).astype(B16)


def triangle(n):
    r = lax.broadcasted_iota(jnp.int32, (n, n), 0)
    c = lax.broadcasted_iota(jnp.int32, (n, n), 1)
    return r >= c


def cumulative(gt, columns):
    low = triangle(gt.shape[1]).astype(F32).astype(B16)
    hi, mid, lo = (
        lax.dot_general(
            low if columns else p,
            p if columns else low,
            (((1,), (1,)), ((), ())),
            preferred_element_type=F32,
        )
        for p in pieces3(gt)
    )
    return hi + (mid + lo)


def decay_rows(d):
    d = jnp.broadcast_to(d, (EXTRA, HEAD_DIM))
    hi, mid, lo = (p.astype(F32) for p in pieces3(d))
    row = lax.broadcasted_iota(jnp.int32, d.shape, 0)
    out = jnp.where(row == 0, hi, jnp.where(row == 1, mid, jnp.where(row == 2, lo, 0.0)))
    return out.astype(B16)


def read_decay(rows):
    r = rows.astype(F32)
    return r[0:1] + (r[1:2] + r[2:3])


def states_kernel(k_hbm, v_hbm, g_hbm, o_hbm, k_ref, v_ref, g_ref, o_ref, sems, out_sems):
    heads = g_ref.shape[0]
    half = o_ref.shape[1] - EXTRA
    cuts = HEAD_DIM // half
    gates, *copies = [
        pltpu.make_async_copy(g_hbm, g_ref, sems.at[0]),
        pltpu.make_async_copy(k_hbm, k_ref, sems.at[1]),
        pltpu.make_async_copy(v_hbm, v_ref, sems.at[2]),
    ]
    for copy in (gates, *copies):
        copy.start()
    gates.wait()
    cum = cumulative(g_ref[...], True)
    last = cum[-1:]
    to_end = jnp.exp(last - cum)
    whole = jnp.exp(last)
    for copy in copies:
        copy.wait()
    leaving = []
    for h in range(heads):
        cols = slice(h * HEAD_DIM, (h + 1) * HEAD_DIM)
        scaled = (k_ref[:, cols].astype(F32) * to_end[:, h : h + 1]).astype(B16)
        state = lax.dot_general(
            scaled, v_ref[:, cols], (((0,), (0,)), ((), ())), preferred_element_type=F32
        ).astype(B16)
        rows = decay_rows(whole[:, h : h + 1])
        for i in range(cuts):
            o_ref[h * cuts + i, :half] = state[i * half : (i + 1) * half]
            o_ref[h * cuts + i, half:] = rows
        part = pl.ds(h * cuts, cuts)
        leaving.append(pltpu.make_async_copy(o_ref.at[part], o_hbm.at[part], out_sems.at[h]))
        leaving[-1].start()
    for copy in leaving:
        copy.wait()


def total_kernel(order, x_ref, o_ref):
    n, rows, _ = x_ref.shape
    half = rows - EXTRA
    for b in range(n):
        at = order.index(b)
        d = read_decay(x_ref[at, half:])
        s = x_ref[at, :half].astype(F32)
        state = d * state + s if b else s
        decay = decay * d if b else d
    state = state.astype(B16)
    tail = decay_rows(decay)
    for j in range(o_ref.shape[0]):
        o_ref[j, :half] = state
        o_ref[j, half:] = tail


def prior_kernel(z_order, order, place_ref, z_ref, x_ref, o_ref):
    place = place_ref[0]
    n, half, _ = o_ref.shape
    state = jnp.zeros((half, HEAD_DIM), F32)
    for j in range(z_ref.shape[0] - 1):
        at = z_order.index(j)
        later = read_decay(z_ref[at, half:]) * state + z_ref[at, :half].astype(F32)
        state = jnp.where(j < place, later, state)
    for b in range(n):
        at = order.index(b)
        o_ref[at] = state.astype(B16)
        if b < n - 1:
            state = read_decay(x_ref[at, half:]) * state + x_ref[at, :half].astype(F32)


def inner_kernel(q_ref, k_ref, v_ref, g_ref, o_ref):
    heads, tok = g_ref.shape
    cum = cumulative(g_ref[...], True)
    cum_t = cumulative(g_ref[...], False)
    causal = triangle(tok)
    for h in range(heads):
        cols = slice(h * HEAD_DIM, (h + 1) * HEAD_DIM)
        scores = lax.dot_general(
            q_ref[:, cols], k_ref[:, cols], (((1,), (1,)), ((), ())), preferred_element_type=F32
        )
        diff = cum[:, h : h + 1] - cum_t[h : h + 1, :]
        factor = jnp.where(causal, jnp.exp(jnp.minimum(diff, 0.0)), 0.0)
        weights = (scores * factor).astype(B16)
        o_ref[:, cols] = jnp.dot(weights, v_ref[:, cols], preferred_element_type=F32)


def output_kernel(order, q_ref, s_ref, i_ref, g_ref, gain_ref, o_ref):
    heads = g_ref.shape[0]
    grown = jnp.exp(cumulative(g_ref[...], True))
    for h in range(heads):
        cols = slice(h * HEAD_DIM, (h + 1) * HEAD_DIM)
        outer = jnp.dot(q_ref[:, cols], s_ref[h], preferred_element_type=F32)
        mixed = i_ref[:, cols] + outer * grown[:, h : h + 1]
        mean = jnp.mean(mixed * mixed, axis=-1, keepdims=True)
        normed = (mixed * lax.rsqrt(mean + 1e-05) * gain_ref[:, cols]).astype(B16)
        quarter = o_ref.shape[1]
        for j, place in enumerate(order):
            o_ref[j, :, cols] = normed[place * quarter : (place + 1) * quarter]


def local(kernel, shape, dtype, *args, flops=0, spaces=(), out=pltpu.VMEM, scratch=(), vmem=32):
    spaces = (*spaces, *(pltpu.VMEM,) * (len(args) - len(spaces)))
    moved = sum(a.size * a.dtype.itemsize for a in args)
    return pl.pallas_call(
        kernel,
        out_shape=jax.ShapeDtypeStruct(shape, dtype),
        in_specs=[pl.BlockSpec(memory_space=space) for space in spaces],
        out_specs=pl.BlockSpec(memory_space=out),
        scratch_shapes=scratch,
        compiler_params=pltpu.CompilerParams(vmem_limit_bytes=vmem * 2**20),
        cost_estimate=pl.CostEstimate(flops=flops, bytes_accessed=moved, transcendentals=0),
    )(*args)


def rotated(n, first):
    return [(first + j) % n for j in range(n)]


def exchange(a, axis, order):
    return lax.all_to_all(a, axis, 0, 0, tiled=True, axis_index_groups=[order])


def body(groups, members, queries, keys, values, log_decay, norm_gain):
    tok, width = queries.shape
    heads = log_decay.shape[1]
    mps = lax.axis_size("mp")
    half = heads * HEAD_DIM // members
    mac = 2 * heads * tok * HEAD_DIM * HEAD_DIM
    z_order = rotated(groups, (5 * groups) // 8)
    order = rotated(members, (13 * members) // 16)
    y_order = rotated(mps, mps // 2)
    gates = log_decay.T
    own = local(
        states_kernel,
        (members, half + EXTRA, HEAD_DIM),
        B16,
        keys,
        values,
        gates,
        flops=mac,
        spaces=(pl.ANY,) * 3,
        out=pl.ANY,
        scratch=[
            pltpu.VMEM((tok, width), B16),
            pltpu.VMEM((tok, width), B16),
            pltpu.VMEM((heads, tok), F32),
            pltpu.VMEM((members, half + EXTRA, HEAD_DIM), B16),
            pltpu.SemaphoreType.DMA((3,)),
            pltpu.SemaphoreType.DMA((heads,)),
        ],
        vmem=60,
    )
    blocks = exchange(own, "g", order)
    total = local(
        functools.partial(total_kernel, order), (groups, half + EXTRA, HEAD_DIM), B16, blocks
    )
    totals = exchange(total, "zh", z_order)
    place = lax.axis_index("zh").astype(jnp.int32).reshape(1)
    prior = local(
        functools.partial(prior_kernel, z_order, order),
        (members, half, HEAD_DIM),
        B16,
        place,
        totals,
        blocks,
        spaces=(pltpu.SMEM,),
    )
    state = exchange(prior, "g", order).reshape(heads, HEAD_DIM, HEAD_DIM)
    inner = local(
        inner_kernel, (tok, width), F32, queries, keys, values, gates, flops=2 * mac
    )
    normed = local(
        functools.partial(output_kernel, y_order),
        (mps, tok // mps, width),
        B16,
        queries,
        state,
        inner,
        gates,
        norm_gain.reshape(1, width),
        flops=mac,
    )
    arrived = exchange(normed, "mp", y_order)
    return jnp.concatenate([arrived[y_order.index(y)] for y in range(mps)], axis=1)


def solution(mesh):
    seq, mp = mesh.devices.shape
    fine = Mesh(mesh.devices.reshape(seq // 16, 16, mp), ("zh", "g", "mp"))
    in_specs = (P(("zh", "g"), "mp"),) * 4 + (P("mp"),)
    return jax.shard_map(
        functools.partial(body, seq // 16, 16),
        mesh=fine,
        in_specs=in_specs,
        out_specs=P(("zh", "g", "mp"), None),
        check_vma=False,
    )
```

time: 74.2 us -> 63.8 us (0.86)
  waiting for transfers between devices: 21.8 us -> 14.6 us
  local copies, waits for them, and re-layouts: 3.42 us -> 0.04 us
  Pallas kernels: 4.53 us -> 6.22 us
  starting transfers between devices: 17.2 us -> 16.1 us
    all_to_all x2, waiting for transfers between devices: 21.8 us -> 14.6 us  [exchange(): return lax.all_to_all(a, axis, 0, 0, tiled=True, axis_index_groups=[order])]
    unnamed x15 -> x10, local copies, waits for them, and re-layouts: 2.7 us -> 0.02 us
    pallas_call x5, Pallas kernels: 4.53 us -> 6.22 us  [local(): pl.pallas_call(kernel, out_shape=jax.ShapeDtypeStruct(shape, dtype), in_s...]
    all_to_all x2, starting transfers between devices: 17.2 us -> 16.1 us  [exchange(): return lax.all_to_all(a, axis, 0, 0, tiled=True, axis_index_groups=[order])]
    all_to_all x2, blocking collectives: 26.3 us -> 25.6 us  [exchange(): return lax.all_to_all(a, axis, 0, 0, tiled=True, axis_index_groups=[order])]
where the time goes in v2:
time: 63.8 us; the launch traced here: 63.4 us
  blocking collectives  25.6 us (40%)
  starting transfers between devices  16.1 us (25%)
  waiting for transfers between devices  14.6 us (23%)
  Pallas kernels  6.22 us (10%)
  other arithmetic  0.72 us (1%)
    all_to_all x2, blocking collectives, exchange(): return lax.all_to_all(a, axis, 0, 0, tiled=True, axis_index_groups=[order])  25.6 us
    all_to_all x2, starting transfers between devices, exchange(): return lax.all_to_all(a, axis, 0, 0, tiled=True, axis_index_groups=[order])  16.1 us
    all_to_all x2, waiting for transfers between devices, exchange(): return lax.all_to_all(a, axis, 0, 0, tiled=True, axis_index_groups=[order])  14.6 us
    pallas_call x5, Pallas kernels, local(): pl.pallas_call(kernel, out_shape=jax.ShapeDtypeStruct(shape, dtype), in_s...  6.22 us
  transfers between devices with their start and end apart: 2, of which 2 were waited for; matrix products, arithmetic and copies ran while one was open for 0% of the time, Pallas kernels for 2%

profile of v2, /device:TPU:6, one launch (start us, length us, event | category | flops | bytes accessed | tf_op | source)
XLA Modules:
  0.0 63.4 jit_solution(13789254342628892877)
XLA Ops:
  0.0 2.3 %shard_map.55 = bf16[16,80,128]{2,1,0:T(8,128)(2,1)} custom-call(bf16[128,1024]{1,0:T(8,128)(2,1)} %k_ref.1, bf16[128,1024]{1,0:T(8,128)(2,1)} %v_ref.1, f32[8,128]{1,0:T(8,128)} %bitcast.13), custom_call_target="tpu_custom_call" | custom-call | flops 33554432 | bytes 528384 | tf_op jit(solution)/shard_map/pallas_call | solution.py:156
  2.3 15.6 %all_to_all.20.x_ref = bf16[16,80,128]{2,1,0:T(8,128)(2,1)S(1)} all-to-all(bf16[16,80,128]{2,1,0:T(8,128)(2,1)} %shard_map.55), channel_id=1, replica_groups={{52,56,60,0,4,8,12,16,20,24,28,32,36,40,44,48},{53,57,61,1,5,9,13,17,21..., dimensions={0} | all-to-all | bytes 655360 | tf_op jit(solution)/shard_map/all_to_all | solution.py:172
  17.9 0.7 %shard_map.56 = bf16[8,80,128]{2,1,0:T(8,128)(2,1)} custom-call(bf16[16,80,128]{2,1,0:T(8,128)(2,1)S(1)} %all_to_all.20.x_ref), custom_call_target="tpu_custom_call" | custom-call | bytes 327680 | tf_op jit(solution)/shard_map/pallas_call | solution.py:156
  18.7 12.1 %all-to-all-start.1 = ((bf16[8,80,128]{2,1,0:T(8,128)(2,1)}), bf16[8,80,128]{2,1,0:T(8,128)(2,1)S(1)}, u32[]{:S(2)}, u32[]{:S(2)}) async-start(bf16[8,80,128]{2,1,0:T(8,128)(2,1)} %shard_map.56), calls=%async_computation.1 | async-start | bytes 327680 | tf_op jit(solution)/shard_map/all_to_all | solution.py:172
  30.8 9.9 %all-to-all-done.1.z_ref = bf16[8,80,128]{2,1,0:T(8,128)(2,1)S(1)} async-done(((bf16[8,80,128]{2,1,0:T(8,128)(2,1)}), bf16[8,80,128]{2,1,0:T(8,128)(2,1)S(1)}, u32[]{:S(2)}, u32[]{:S(2)}) %all-to-all-start.1) | async-done | bytes 163872 | tf_op jit(solution)/shard_map/all_to_all | solution.py:172
  40.7 0.0 copy-start.2
  40.7 0.0 copy-start.3
  40.7 0.8 %shard_map.57 = bf16[16,64,128]{2,1,0:T(8,128)(2,1)} custom-call(s32[1]{0:T(128)} %bitcast.place_ref, bf16[8,80,128]{2,1,0:T(8,128)(2,1)S(1)} %all-to-all-done.1.z_ref, bf16[16,80,128]{2,1,0:T(8,128)(2,1)S(1)} %all_to_all.20.x_ref), custom_call_target="tpu_custom_call" | custom-call | bytes 491524 | tf_op jit(solution)/shard_map/pallas_call | solution.py:156
  41.5 0.0 copy-start
  41.5 0.0 copy-start.1
  41.5 4.1 %all-to-all-start.2 = ((bf16[16,64,128]{2,1,0:T(8,128)(2,1)}), bf16[16,64,128]{2,1,0:T(8,128)(2,1)S(1)}, u32[]{:S(2)}, u32[]{:S(2)}) async-start(bf16[16,64,128]{2,1,0:T(8,128)(2,1)} %shard_map.57), calls=%async_computation.2 | async-start | bytes 524288 | tf_op jit(solution)/shard_map/all_to_all | solution.py:172
  45.5 0.0 copy-done.2
  45.5 0.0 copy-done.3
  45.6 0.0 copy-done
  45.6 0.0 copy-done.1
  45.6 0.0 copy-start.4
  45.6 1.4 %shard_map.58.i_ref = f32[128,1024]{1,0:T(8,128)S(1)} custom-call(bf16[128,1024]{1,0:T(8,128)(2,1)S(1)} %copy-done, bf16[128,1024]{1,0:T(8,128)(2,1)S(1)} %copy-done.1, bf16[128,1024]{1,0:T(8,128)(2,1)S(1)} %copy-done.2, f32[8,128]{1,0:T(8,128)S(1)} %bitcast.14), custom_call_target="tpu_custom_call" | custom-call | flops 67108864 | bytes 790528 | tf_op jit(solution)/shard_map/pallas_call | solution.py:156
  47.0 4.7 %all-to-all-done.2 = bf16[16,64,128]{2,1,0:T(8,128)(2,1)S(1)} async-done(((bf16[16,64,128]{2,1,0:T(8,128)(2,1)}), bf16[16,64,128]{2,1,0:T(8,128)(2,1)S(1)}, u32[]{:S(2)}, u32[]{:S(2)}) %all-to-all-start.2) | async-done | bytes 262176 | tf_op jit(solution)/shard_map/all_to_all | solution.py:172
  51.8 0.0 copy-done.4
  51.8 0.9 %shard_map.59 = bf16[4,32,1024]{2,1,0:T(8,128)(2,1)S(1)} custom-call(bf16[128,1024]{1,0:T(8,128)(2,1)S(1)} %copy-done, bf16[8,128,128]{2,1,0:T(8,128)(2,1)S(1)} %bitcast.12, f32[128,1024]{1,0:T(8,128)S(1)} %shard_map.58.i_ref, f32[8,128]{1,0:T(8,128)S(1)} %bitcast.15, f32[1,1024]{1,0:T(1,128)S(1)} %bitcast.16), custom_call_target="tpu_custom_call" | custom-call | flops 33554432 | bytes 1056768 | tf_op jit(solution)/shard_map/pallas_call | solution.py:156
  52.7 10.0 %all_to_all.21 = bf16[4,32,1024]{2,1,0:T(8,128)(2,1)S(1)} all-to-all(bf16[4,32,1024]{2,1,0:T(8,128)(2,1)S(1)} %shard_map.59), channel_id=1, replica_groups={{2,3,0,1},{6,7,4,5},{10,11,8,9},{14,15,12,13},{18,19,16,17},{22,23,20,2..., dimensions={0} | all-to-all | bytes 524288 | tf_op jit(solution)/shard_map/all_to_all | solution.py:172
  62.7 0.7 %pad_maximum_fusion = bf16[32,4096]{1,0:T(8,128)(2,1)} fusion(bf16[32,1024]{1,0:T(8,128)(2,1)S(1)} %get-tuple-element.6, bf16[32,1024]{1,0:T(8,128)(2,1)S(1)} %get-tuple-element.7, bf16[32,1024]{1,0:T(8,128)(2,1)S(1)} %get-tuple-element.8, bf16[32,1024]{1,0:T(8,128)(2,1)S(1)} %get-tuple-element.5), kind=kLoop, calls=%fused_computation | loop fusion | flops 1048576 | bytes 524288 | tf_op jit(solution)/shard_map/concatenate | solution.py:236
  (1 shorter events, 0.0 us)
Async XLA Ops:
  18.7 22.0 %all-to-all-start.1 = ((bf16[8,80,128]{2,1,0:T(8,128)(2,1)}), bf16[8,80,128]{2,1,0:T(8,128)(2,1)S(1)}, u32[]{:S(2)}, u32[]{:S(2)}) async-start(bf16[8,80,128]{2,1,0:T(8,128)(2,1)} %shard_map.56), calls=%async_computation.1 | async-start | bytes 327680 | tf_op jit(solution)/shard_map/all_to_all | solution.py:172
  40.7 4.9 %copy-start.2 = (bf16[128,1024]{1,0:T(8,128)(2,1)S(1)}, bf16[128,1024]{1,0:T(8,128)(2,1)}, u32[]{:S(2)}) copy-start(bf16[128,1024]{1,0:T(8,128)(2,1)} %v_ref.1) | copy-start | bytes 786436
  40.7 4.9 %copy-start.3 = (f32[128,8]{0,1:T(8,128)S(1)}, f32[128,8]{0,1:T(8,128)}, u32[]{:S(2)}) copy-start(f32[128,8]{0,1:T(8,128)} %param.8) | copy-start | bytes 12292
  41.5 4.1 %copy-start = (bf16[128,1024]{1,0:T(8,128)(2,1)S(1)}, bf16[128,1024]{1,0:T(8,128)(2,1)}, u32[]{:S(2)}) copy-start(bf16[128,1024]{1,0:T(8,128)(2,1)} %q_ref.3) | copy-start | bytes 786436
  41.5 4.1 %copy-start.1 = (bf16[128,1024]{1,0:T(8,128)(2,1)S(1)}, bf16[128,1024]{1,0:T(8,128)(2,1)}, u32[]{:S(2)}) copy-start(bf16[128,1024]{1,0:T(8,128)(2,1)} %k_ref.1) | copy-start | bytes 786436
  41.5 10.3 %all-to-all-start.2 = ((bf16[16,64,128]{2,1,0:T(8,128)(2,1)}), bf16[16,64,128]{2,1,0:T(8,128)(2,1)S(1)}, u32[]{:S(2)}, u32[]{:S(2)}) async-start(bf16[16,64,128]{2,1,0:T(8,128)(2,1)} %shard_map.57), calls=%async_computation.2 | async-start | bytes 524288 | tf_op jit(solution)/shard_map/all_to_all | solution.py:172
  45.6 6.2 %copy-start.4 = (f32[1024]{0:T(1024)S(1)}, f32[1024]{0:T(1024)}, u32[]{:S(2)}) copy-start(f32[1024]{0:T(1024)} %param.9) | copy-start | bytes 12292

commit v3 on v2

--- a/solution.py
+++ b/solution.py
@@ -10,7 +10,7 @@
 HEAD_DIM = 128
 F32 = jnp.float32
 B16 = jnp.bfloat16
-EXTRA = 16
+EXTRA = 8
 
 
 def pieces3(a):
@@ -178,7 +178,8 @@
     mps = lax.axis_size("mp")
     half = heads * HEAD_DIM // members
     mac = 2 * heads * tok * HEAD_DIM * HEAD_DIM
-    z_order = rotated(groups, (5 * groups) // 8)
+    z_order = [(5 * groups) // 8]
+    z_order += [z for z in range(groups)[::-1] if z not in z_order]
     order = rotated(members, (13 * members) // 16)
     y_order = rotated(mps, mps // 2)
     gates = log_decay.T
@@ -208,6 +209,10 @@
     )
     totals = exchange(total, "zh", z_order)
     place = lax.axis_index("zh").astype(jnp.int32).reshape(1)
+    inner = local(
+        inner_kernel, (tok, width), F32, queries, keys, values, gates, flops=2 * mac
+    )
+    totals, inner = lax.optimization_barrier((totals, inner))
     prior = local(
         functools.partial(prior_kernel, z_order, order),
         (members, half, HEAD_DIM),
@@ -218,9 +223,6 @@
         spaces=(pltpu.SMEM,),
     )
     state = exchange(prior, "g", order).reshape(heads, HEAD_DIM, HEAD_DIM)
-    inner = local(
-        inner_kernel, (tok, width), F32, queries, keys, values, gates, flops=2 * mac
-    )
     normed = local(
         functools.partial(output_kernel, y_order),
         (mps, tok // mps, width),

time: 63.8 us -> 60.9 us (0.955)
  blocking collectives: 25.6 us -> 35.3 us
  waiting for transfers between devices: 14.6 us -> 6.13 us
  starting transfers between devices: 16.1 us -> 12.1 us
  Pallas kernels: 6.22 us -> 5.51 us
  local copies, waits for them, and re-layouts: 0.04 us -> 0.71 us
    all_to_all x2 -> x3, blocking collectives: 25.6 us -> 35.3 us  [exchange(): return lax.all_to_all(a, axis, 0, 0, tiled=True, axis_index_groups=[order])]
    all_to_all x2 -> x1, waiting for transfers between devices: 14.6 us -> 6.13 us  [exchange(): return lax.all_to_all(a, axis, 0, 0, tiled=True, axis_index_groups=[order])]
    all_to_all x2 -> x1, starting transfers between devices: 16.1 us -> 12.1 us  [exchange(): return lax.all_to_all(a, axis, 0, 0, tiled=True, axis_index_groups=[order])]
    pallas_call x5, Pallas kernels: 6.22 us -> 5.51 us  [local(): pl.pallas_call(kernel, out_shape=jax.ShapeDtypeStruct(shape, dtype), in_s...]
    unnamed x10, local copies, waits for them, and re-layouts: 0.02 us -> 0.69 us
  transfers between devices with their start and end apart: 2 -> 1, of which waited for: 2 -> 1; matrix products, arithmetic and copies ran while one was open for 0% -> 0% of each run, Pallas kernels for 2% -> 2%
where the time goes in v3:
time: 60.9 us; the launch traced here: 60.5 us
  blocking collectives  35.3 us (58%)
  starting transfers between devices  12.1 us (20%)
  waiting for transfers between devices  6.13 us (10%)
  Pallas kernels  5.51 us (9%)
  other arithmetic  0.72 us (1%)
  local copies, waits for them, and re-layouts  0.71 us (1%)
    all_to_all x3, blocking collectives, exchange(): return lax.all_to_all(a, axis, 0, 0, tiled=True, axis_index_groups=[order])  35.3 us
    all_to_all x1, starting transfers between devices, exchange(): return lax.all_to_all(a, axis, 0, 0, tiled=True, axis_index_groups=[order])  12.1 us
    all_to_all x1, waiting for transfers between devices, exchange(): return lax.all_to_all(a, axis, 0, 0, tiled=True, axis_index_groups=[order])  6.13 us
    pallas_call x5, Pallas kernels, local(): pl.pallas_call(kernel, out_shape=jax.ShapeDtypeStruct(shape, dtype), in_s...  5.51 us
  transfers between devices with their start and end apart: 1, of which 1 were waited for; matrix products, arithmetic and copies ran while one was open for 0% of the time, Pallas kernels for 2%

profile of v3, /device:TPU:6, one launch (start us, length us, event | category | flops | bytes accessed | tf_op | source)
XLA Modules:
  0.0 60.5 jit_solution(17639679866782299205)
XLA Ops:
  0.0 2.3 %shard_map.55 = bf16[16,72,128]{2,1,0:T(8,128)(2,1)} custom-call(bf16[128,1024]{1,0:T(8,128)(2,1)} %k_ref.1, bf16[128,1024]{1,0:T(8,128)(2,1)} %v_ref.1, f32[8,128]{1,0:T(8,128)} %bitcast.13), custom_call_target="tpu_custom_call" | custom-call | flops 33554432 | bytes 528384 | tf_op jit(solution)/shard_map/pallas_call | solution.py:156
  2.3 0.0 copy-start.2
  2.4 15.4 %all_to_all.20.x_ref = bf16[16,72,128]{2,1,0:T(8,128)(2,1)S(1)} all-to-all(bf16[16,72,128]{2,1,0:T(8,128)(2,1)} %shard_map.55), channel_id=1, replica_groups={{52,56,60,0,4,8,12,16,20,24,28,32,36,40,44,48},{53,57,61,1,5,9,13,17,21..., dimensions={0} | all-to-all | bytes 589824 | tf_op jit(solution)/shard_map/all_to_all | solution.py:172
  17.7 0.0 copy-start
  17.7 0.0 copy-start.1
  17.7 0.7 %shard_map.56 = bf16[8,72,128]{2,1,0:T(8,128)(2,1)} custom-call(bf16[16,72,128]{2,1,0:T(8,128)(2,1)S(1)} %all_to_all.20.x_ref), custom_call_target="tpu_custom_call" | custom-call | bytes 294912 | tf_op jit(solution)/shard_map/pallas_call | solution.py:156
  18.5 12.1 %all-to-all-start.1 = ((bf16[8,72,128]{2,1,0:T(8,128)(2,1)}), bf16[8,72,128]{2,1,0:T(8,128)(2,1)S(1)}, u32[]{:S(2)}, u32[]{:S(2)}) async-start(bf16[8,72,128]{2,1,0:T(8,128)(2,1)} %shard_map.56), calls=%async_computation.1 | async-start | bytes 294912 | tf_op jit(solution)/shard_map/all_to_all | solution.py:172
  30.5 0.0 copy-start.3
  30.5 0.0 copy-done.2
  30.5 0.0 copy-done
  30.5 0.0 copy-done.1
  30.6 0.7 %copy-done.3 = f32[128,8]{0,1:T(8,128)S(1)} copy-done((f32[128,8]{0,1:T(8,128)S(1)}, f32[128,8]{0,1:T(8,128)}, u32[]{:S(2)}) %copy-start.3) | copy-done | bytes 4120
  31.2 1.4 %shard_map.57.i_ref = f32[128,1024]{1,0:T(8,128)S(1)} custom-call(bf16[128,1024]{1,0:T(8,128)(2,1)S(1)} %copy-done.2, bf16[128,1024]{1,0:T(8,128)(2,1)S(1)} %copy-done, bf16[128,1024]{1,0:T(8,128)(2,1)S(1)} %copy-done.1, f32[8,128]{1,0:T(8,128)S(1)} %bitcast.14), custom_call_target="tpu_custom_call" | custom-call | flops 67108864 | bytes 790528 | tf_op jit(solution)/shard_map/pallas_call | solution.py:156
  32.7 6.1 %all-to-all-done.1.z_ref = bf16[8,72,128]{2,1,0:T(8,128)(2,1)S(1)} async-done(((bf16[8,72,128]{2,1,0:T(8,128)(2,1)}), bf16[8,72,128]{2,1,0:T(8,128)(2,1)S(1)}, u32[]{:S(2)}, u32[]{:S(2)}) %all-to-all-start.1) | async-done | bytes 147488 | tf_op jit(solution)/shard_map/all_to_all | solution.py:172
  38.8 0.1 shard_map.58
  38.9 0.0 copy-start.4
  38.9 10.0 %all_to_all.21 = bf16[16,64,128]{2,1,0:T(8,128)(2,1)S(1)} all-to-all(bf16[16,64,128]{2,1,0:T(8,128)(2,1)S(1)} %shard_map.58), channel_id=1, replica_groups={{52,56,60,0,4,8,12,16,20,24,28,32,36,40,44,48},{53,57,61,1,5,9,13,17,21..., dimensions={0} | all-to-all | bytes 524288 | tf_op jit(solution)/shard_map/all_to_all | solution.py:172
  48.9 0.0 copy-done.4
  48.9 0.9 %shard_map.59 = bf16[4,32,1024]{2,1,0:T(8,128)(2,1)S(1)} custom-call(bf16[128,1024]{1,0:T(8,128)(2,1)S(1)} %copy-done.2, bf16[8,128,128]{2,1,0:T(8,128)(2,1)S(1)} %bitcast.12, f32[128,1024]{1,0:T(8,128)S(1)} %shard_map.57.i_ref, f32[8,128]{1,0:T(8,128)S(1)} %bitcast.15, f32[1,1024]{1,0:T(1,128)S(1)} %bitcast.16), custom_call_target="tpu_custom_call" | custom-call | flops 33554432 | bytes 1056768 | tf_op jit(solution)/shard_map/pallas_call | solution.py:156
  49.8 10.0 %all_to_all.22 = bf16[4,32,1024]{2,1,0:T(8,128)(2,1)S(1)} all-to-all(bf16[4,32,1024]{2,1,0:T(8,128)(2,1)S(1)} %shard_map.59), channel_id=1, replica_groups={{2,3,0,1},{6,7,4,5},{10,11,8,9},{14,15,12,13},{18,19,16,17},{22,23,20,2..., dimensions={0} | all-to-all | bytes 524288 | tf_op jit(solution)/shard_map/all_to_all | solution.py:172
  59.8 0.7 %pad_maximum_fusion = bf16[32,4096]{1,0:T(8,128)(2,1)} fusion(bf16[32,1024]{1,0:T(8,128)(2,1)S(1)} %get-tuple-element.10, bf16[32,1024]{1,0:T(8,128)(2,1)S(1)} %get-tuple-element.11, bf16[32,1024]{1,0:T(8,128)(2,1)S(1)} %get-tuple-element.12, bf16[32,1024]{1,0:T(8,128)(2,1)S(1)} %get-tuple-element.9), kind=kLoop, calls=%fused_computation | loop fusion | flops 1048576 | bytes 524288 | tf_op jit(solution)/shard_map/concatenate | solution.py:238
  (1 shorter events, 0.0 us)
Async XLA Ops:
  2.3 28.2 %copy-start.2 = (bf16[128,1024]{1,0:T(8,128)(2,1)S(1)}, bf16[128,1024]{1,0:T(8,128)(2,1)}, u32[]{:S(2)}) copy-start(bf16[128,1024]{1,0:T(8,128)(2,1)} %q_ref.3) | copy-start | bytes 786436
  17.7 12.8 %copy-start = (bf16[128,1024]{1,0:T(8,128)(2,1)S(1)}, bf16[128,1024]{1,0:T(8,128)(2,1)}, u32[]{:S(2)}) copy-start(bf16[128,1024]{1,0:T(8,128)(2,1)} %k_ref.1) | copy-start | bytes 786436
  17.7 12.8 %copy-start.1 = (bf16[128,1024]{1,0:T(8,128)(2,1)S(1)}, bf16[128,1024]{1,0:T(8,128)(2,1)}, u32[]{:S(2)}) copy-start(bf16[128,1024]{1,0:T(8,128)(2,1)} %v_ref.1) | copy-start | bytes 786436
  18.5 20.3 %all-to-all-start.1 = ((bf16[8,72,128]{2,1,0:T(8,128)(2,1)}), bf16[8,72,128]{2,1,0:T(8,128)(2,1)S(1)}, u32[]{:S(2)}, u32[]{:S(2)}) async-start(bf16[8,72,128]{2,1,0:T(8,128)(2,1)} %shard_map.56), calls=%async_computation.1 | async-start | bytes 294912 | tf_op jit(solution)/shard_map/all_to_all | solution.py:172
  30.5 0.7 %copy-start.3 = (f32[128,8]{0,1:T(8,128)S(1)}, f32[128,8]{0,1:T(8,128)}, u32[]{:S(2)}) copy-start(f32[128,8]{0,1:T(8,128)} %param.8) | copy-start | bytes 12292
  38.9 10.0 %copy-start.4 = (f32[1024]{0:T(1024)S(1)}, f32[1024]{0:T(1024)}, u32[]{:S(2)}) copy-start(f32[1024]{0:T(1024)} %param.9) | copy-start | bytes 12292

commit v4 on v3

--- a/solution.py
+++ b/solution.py
@@ -89,12 +89,13 @@
         copy.wait()
 
 
-def total_kernel(order, x_ref, o_ref):
+def total_kernel(order, x_ref, o_ref, d_ref):
     n, rows, _ = x_ref.shape
     half = rows - EXTRA
     for b in range(n):
         at = order.index(b)
         d = read_decay(x_ref[at, half:])
+        d_ref[b : b + 1] = d
         s = x_ref[at, :half].astype(F32)
         state = d * state + s if b else s
         decay = decay * d if b else d
@@ -105,7 +106,7 @@
         o_ref[j, half:] = tail
 
 
-def prior_kernel(z_order, order, place_ref, z_ref, x_ref, o_ref):
+def prior_kernel(z_order, order, place_ref, z_ref, x_ref, d_ref, o_ref):
     place = place_ref[0]
     n, half, _ = o_ref.shape
     state = jnp.zeros((half, HEAD_DIM), F32)
@@ -117,13 +118,14 @@
         at = order.index(b)
         o_ref[at] = state.astype(B16)
         if b < n - 1:
-            state = read_decay(x_ref[at, half:]) * state + x_ref[at, :half].astype(F32)
-
-
-def inner_kernel(q_ref, k_ref, v_ref, g_ref, o_ref):
+            state = d_ref[b : b + 1] * state + x_ref[at, :half].astype(F32)
+
+
+def inner_kernel(q_ref, k_ref, v_ref, g_ref, o_ref, e_ref):
     heads, tok = g_ref.shape
     cum = cumulative(g_ref[...], True)
     cum_t = cumulative(g_ref[...], False)
+    e_ref[...] = jnp.exp(cum)
     causal = triangle(tok)
     for h in range(heads):
         cols = slice(h * HEAD_DIM, (h + 1) * HEAD_DIM)
@@ -136,9 +138,9 @@
         o_ref[:, cols] = jnp.dot(weights, v_ref[:, cols], preferred_element_type=F32)
 
 
-def output_kernel(order, q_ref, s_ref, i_ref, g_ref, gain_ref, o_ref):
-    heads = g_ref.shape[0]
-    grown = jnp.exp(cumulative(g_ref[...], True))
+def output_kernel(order, q_ref, s_ref, i_ref, e_ref, gain_ref, o_ref):
+    heads = e_ref.shape[1]
+    grown = e_ref[...]
     for h in range(heads):
         cols = slice(h * HEAD_DIM, (h + 1) * HEAD_DIM)
         outer = jnp.dot(q_ref[:, cols], s_ref[h], preferred_element_type=F32)
@@ -150,14 +152,14 @@
             o_ref[j, :, cols] = normed[place * quarter : (place + 1) * quarter]
 
 
-def local(kernel, shape, dtype, *args, flops=0, spaces=(), out=pltpu.VMEM, scratch=(), vmem=32):
+def local(kernel, outs, *args, flops=0, spaces=(), out=pltpu.VMEM, scratch=(), vmem=32):
     spaces = (*spaces, *(pltpu.VMEM,) * (len(args) - len(spaces)))
     moved = sum(a.size * a.dtype.itemsize for a in args)
     return pl.pallas_call(
         kernel,
-        out_shape=jax.ShapeDtypeStruct(shape, dtype),
+        out_shape=[jax.ShapeDtypeStruct(shape, dtype) for shape, dtype in outs],
         in_specs=[pl.BlockSpec(memory_space=space) for space in spaces],
-        out_specs=pl.BlockSpec(memory_space=out),
+        out_specs=[pl.BlockSpec(memory_space=out)] * len(outs),
         scratch_shapes=scratch,
         compiler_params=pltpu.CompilerParams(vmem_limit_bytes=vmem * 2**20),
         cost_estimate=pl.CostEstimate(flops=flops, bytes_accessed=moved, transcendentals=0),
@@ -183,10 +185,9 @@
     order = rotated(members, (13 * members) // 16)
     y_order = rotated(mps, mps // 2)
     gates = log_decay.T
-    own = local(
+    (own,) = local(
         states_kernel,
-        (members, half + EXTRA, HEAD_DIM),
-        B16,
+        [((members, half + EXTRA, HEAD_DIM), B16)],
         keys,
         values,
         gates,
@@ -204,33 +205,40 @@
         vmem=60,
     )
     blocks = exchange(own, "g", order)
-    total = local(
-        functools.partial(total_kernel, order), (groups, half + EXTRA, HEAD_DIM), B16, blocks
+    total, decays = local(
+        functools.partial(total_kernel, order),
+        [((groups, half + EXTRA, HEAD_DIM), B16), ((members, HEAD_DIM), F32)],
+        blocks,
     )
     totals = exchange(total, "zh", z_order)
     place = lax.axis_index("zh").astype(jnp.int32).reshape(1)
-    inner = local(
-        inner_kernel, (tok, width), F32, queries, keys, values, gates, flops=2 * mac
-    )
-    totals, inner = lax.optimization_barrier((totals, inner))
-    prior = local(
+    inner, grown = local(
+        inner_kernel,
+        [((tok, width), F32), ((tok, heads), F32)],
+        queries,
+        keys,
+        values,
+        gates,
+        flops=2 * mac,
+    )
+    totals, inner, grown = lax.optimization_barrier((totals, inner, grown))
+    (prior,) = local(
         functools.partial(prior_kernel, z_order, order),
-        (members, half, HEAD_DIM),
-        B16,
+        [((members, half, HEAD_DIM), B16)],
         place,
         totals,
         blocks,
+        decays,
         spaces=(pltpu.SMEM,),
     )
     state = exchange(prior, "g", order).reshape(heads, HEAD_DIM, HEAD_DIM)
-    normed = local(
+    (normed,) = local(
         functools.partial(output_kernel, y_order),
-        (mps, tok // mps, width),
-        B16,
+        [((mps, tok // mps, width), B16)],
         queries,
         state,
         inner,
-        gates,
+        grown,
         norm_gain.reshape(1, width),
         flops=mac,
     )

time: 60.9 us -> 60.8 us (level)
  no operation moved by 1% of the time
where the time goes in v4:
time: 60.8 us; the launch traced here: 60.4 us
  blocking collectives  35.3 us (58%)
  starting transfers between devices  12.1 us (20%)
  waiting for transfers between devices  6.13 us (10%)
  Pallas kernels  5.39 us (9%)
  other arithmetic  0.72 us (1%)
  local copies, waits for them, and re-layouts  0.71 us (1%)
    all_to_all x3, blocking collectives, exchange(): return lax.all_to_all(a, axis, 0, 0, tiled=True, axis_index_groups=[order])  35.3 us
    all_to_all x1, starting transfers between devices, exchange(): return lax.all_to_all(a, axis, 0, 0, tiled=True, axis_index_groups=[order])  12.1 us
    all_to_all x1, waiting for transfers between devices, exchange(): return lax.all_to_all(a, axis, 0, 0, tiled=True, axis_index_groups=[order])  6.13 us
    pallas_call x5, Pallas kernels, local(): pl.pallas_call(kernel, out_shape=[jax.ShapeDtypeStruct(shape, dtype) for...  5.39 us
  transfers between devices with their start and end apart: 1, of which 1 were waited for; matrix products, arithmetic and copies ran while one was open for 0% of the time, Pallas kernels for 2%

profile of v4, /device:TPU:6, one launch (start us, length us, event | category | flops | bytes accessed | tf_op | source)
XLA Modules:
  0.0 60.4 jit_solution(2712202796302282145)
XLA Ops:
  0.0 2.3 %shard_map.55 = bf16[16,72,128]{2,1,0:T(8,128)(2,1)} custom-call(bf16[128,1024]{1,0:T(8,128)(2,1)} %k_ref.1, bf16[128,1024]{1,0:T(8,128)(2,1)} %v_ref.1, f32[8,128]{1,0:T(8,128)} %bitcast.13), custom_call_target="tpu_custom_call" | custom-call | flops 33554432 | bytes 528384 | tf_op jit(solution)/shard_map/pallas_call | solution.py:158
  2.4 0.0 copy-start.2
  2.4 15.4 %all_to_all.20.x_ref = bf16[16,72,128]{2,1,0:T(8,128)(2,1)S(1)} all-to-all(bf16[16,72,128]{2,1,0:T(8,128)(2,1)} %shard_map.55), channel_id=1, replica_groups={{52,56,60,0,4,8,12,16,20,24,28,32,36,40,44,48},{53,57,61,1,5,9,13,17,21..., dimensions={0} | all-to-all | bytes 589824 | tf_op jit(solution)/shard_map/all_to_all | solution.py:174
  17.7 0.0 copy-start
  17.7 0.0 copy-start.1
  17.7 0.7 %shard_map.56 = (bf16[8,72,128]{2,1,0:T(8,128)(2,1)}, f32[16,128]{1,0:T(8,128)S(1)}) custom-call(bf16[16,72,128]{2,1,0:T(8,128)(2,1)S(1)} %all_to_all.20.x_ref), custom_call_target="tpu_custom_call" | custom-call | bytes 294912 | tf_op jit(solution)/shard_map/pallas_call | solution.py:158
  18.5 12.1 %all-to-all-start.1 = ((bf16[8,72,128]{2,1,0:T(8,128)(2,1)}), bf16[8,72,128]{2,1,0:T(8,128)(2,1)S(1)}, u32[]{:S(2)}, u32[]{:S(2)}) async-start(bf16[8,72,128]{2,1,0:T(8,128)(2,1)} %get-tuple-element.12), calls=%async_computation.1 | async-start | bytes 294912 | tf_op jit(solution)/shard_map/all_to_all | solution.py:174
  30.5 0.0 copy-start.3
  30.5 0.0 copy-done.2
  30.5 0.0 copy-done
  30.6 0.0 copy-done.1
  30.6 0.7 %copy-done.3 = f32[128,8]{0,1:T(8,128)S(1)} copy-done((f32[128,8]{0,1:T(8,128)S(1)}, f32[128,8]{0,1:T(8,128)}, u32[]{:S(2)}) %copy-start.3) | copy-done | bytes 4120
  31.2 1.4 %shard_map.57 = (f32[128,1024]{1,0:T(8,128)S(1)}, f32[128,8]{1,0:T(8,128)S(1)}) custom-call(bf16[128,1024]{1,0:T(8,128)(2,1)S(1)} %copy-done.2, bf16[128,1024]{1,0:T(8,128)(2,1)S(1)} %copy-done, bf16[128,1024]{1,0:T(8,128)(2,1)S(1)} %copy-done.1, f32[8,128]{1,0:T(8,128)S(1)} %bitcast.14), custom_call_target="tpu_custom_call" | custom-call | flops 67108864 | bytes 790528 | tf_op jit(solution)/shard_map/pallas_call | solution.py:158
  32.7 6.1 %all-to-all-done.1.z_ref = bf16[8,72,128]{2,1,0:T(8,128)(2,1)S(1)} async-done(((bf16[8,72,128]{2,1,0:T(8,128)(2,1)}), bf16[8,72,128]{2,1,0:T(8,128)(2,1)S(1)}, u32[]{:S(2)}, u32[]{:S(2)}) %all-to-all-start.1) | async-done | bytes 147488 | tf_op jit(solution)/shard_map/all_to_all | solution.py:174
  38.8 0.1 shard_map.58
  38.9 0.0 copy-start.4
  38.9 10.0 %all_to_all.21 = bf16[16,64,128]{2,1,0:T(8,128)(2,1)S(1)} all-to-all(bf16[16,64,128]{2,1,0:T(8,128)(2,1)S(1)} %shard_map.58), channel_id=1, replica_groups={{52,56,60,0,4,8,12,16,20,24,28,32,36,40,44,48},{53,57,61,1,5,9,13,17,21..., dimensions={0} | all-to-all | bytes 524288 | tf_op jit(solution)/shard_map/all_to_all | solution.py:174
  48.9 0.0 copy-done.4
  48.9 0.8 %shard_map.59 = bf16[4,32,1024]{2,1,0:T(8,128)(2,1)S(1)} custom-call(bf16[128,1024]{1,0:T(8,128)(2,1)S(1)} %copy-done.2, bf16[8,128,128]{2,1,0:T(8,128)(2,1)S(1)} %bitcast.12, f32[128,1024]{1,0:T(8,128)S(1)} %get-tuple-element.17.i_ref, f32[128,8]{1,0:T(8,128)S(1)} %get-tuple-element.18.e_ref, f32[1,1024]{1,0:T(1,128)S(1)} %bitcast.15), custom_call_target="tpu_custom_call" | custom-call | flops 33554432 | bytes 1056768 | tf_op jit(solution)/shard_map/pallas_call | solution.py:158
  49.7 10.0 %all_to_all.22 = bf16[4,32,1024]{2,1,0:T(8,128)(2,1)S(1)} all-to-all(bf16[4,32,1024]{2,1,0:T(8,128)(2,1)S(1)} %shard_map.59), channel_id=1, replica_groups={{2,3,0,1},{6,7,4,5},{10,11,8,9},{14,15,12,13},{18,19,16,17},{22,23,20,2..., dimensions={0} | all-to-all | bytes 524288 | tf_op jit(solution)/shard_map/all_to_all | solution.py:174
  59.7 0.7 %pad_maximum_fusion = bf16[32,4096]{1,0:T(8,128)(2,1)} fusion(bf16[32,1024]{1,0:T(8,128)(2,1)S(1)} %get-tuple-element.20, bf16[32,1024]{1,0:T(8,128)(2,1)S(1)} %get-tuple-element.21, bf16[32,1024]{1,0:T(8,128)(2,1)S(1)} %get-tuple-element.22, bf16[32,1024]{1,0:T(8,128)(2,1)S(1)} %get-tuple-element.19), kind=kLoop, calls=%fused_computation | loop fusion | flops 1048576 | bytes 524288 | tf_op jit(solution)/shard_map/concatenate | solution.py:246
  (1 shorter events, 0.0 us)
Async XLA Ops:
  2.4 28.2 %copy-start.2 = (bf16[128,1024]{1,0:T(8,128)(2,1)S(1)}, bf16[128,1024]{1,0:T(8,128)(2,1)}, u32[]{:S(2)}) copy-start(bf16[128,1024]{1,0:T(8,128)(2,1)} %q_ref.3) | copy-start | bytes 786436
  17.7 12.8 %copy-start = (bf16[128,1024]{1,0:T(8,128)(2,1)S(1)}, bf16[128,1024]{1,0:T(8,128)(2,1)}, u32[]{:S(2)}) copy-start(bf16[128,1024]{1,0:T(8,128)(2,1)} %k_ref.1) | copy-start | bytes 786436
  17.7 12.8 %copy-start.1 = (bf16[128,1024]{1,0:T(8,128)(2,1)S(1)}, bf16[128,1024]{1,0:T(8,128)(2,1)}, u32[]{:S(2)}) copy-start(bf16[128,1024]{1,0:T(8,128)(2,1)} %v_ref.1) | copy-start | bytes 786436
  18.5 20.3 %all-to-all-start.1 = ((bf16[8,72,128]{2,1,0:T(8,128)(2,1)}), bf16[8,72,128]{2,1,0:T(8,128)(2,1)S(1)}, u32[]{:S(2)}, u32[]{:S(2)}) async-start(bf16[8,72,128]{2,1,0:T(8,128)(2,1)} %get-tuple-element.12), calls=%async_computation.1 | async-start | bytes 294912 | tf_op jit(solution)/shard_map/all_to_all | solution.py:174
  30.5 0.7 %copy-start.3 = (f32[128,8]{0,1:T(8,128)S(1)}, f32[128,8]{0,1:T(8,128)}, u32[]{:S(2)}) copy-start(f32[128,8]{0,1:T(8,128)} %param.8) | copy-start | bytes 12292
  38.9 10.0 %copy-start.4 = (f32[1024]{0:T(1024)S(1)}, f32[1024]{0:T(1024)}, u32[]{:S(2)}) copy-start(f32[1024]{0:T(1024)} %param.9) | copy-start | bytes 12292

commit v5 on v4

--- a/solution.py
+++ b/solution.py
@@ -106,14 +106,26 @@
         o_ref[j, half:] = tail
 
 
-def prior_kernel(z_order, order, place_ref, z_ref, x_ref, d_ref, o_ref):
-    place = place_ref[0]
+def half_kernel(z_order, z_ref, o_ref):
+    half = o_ref.shape[0]
+    state = jnp.zeros((half, HEAD_DIM), F32)
+    for j in range(z_ref.shape[0]):
+        at = z_order.index(j)
+        state = read_decay(z_ref[at, half:]) * state + z_ref[at, :half].astype(F32)
+    o_ref[...] = state.astype(B16)
+
+
+def prior_kernel(low_order, high_order, order, place_ref, low_ref, high_ref, first_ref, x_ref, d_ref, o_ref):
     n, half, _ = o_ref.shape
-    state = jnp.zeros((half, HEAD_DIM), F32)
-    for j in range(z_ref.shape[0] - 1):
-        at = z_order.index(j)
-        later = read_decay(z_ref[at, half:]) * state + z_ref[at, :half].astype(F32)
-        state = jnp.where(j < place, later, state)
+    count = low_ref.shape[0]
+    late = place_ref[0] >= count
+    place = lax.rem(place_ref[0], count)
+    state = jnp.where(late, first_ref[...].astype(F32), 0.0)
+    for j in range(count - 1):
+        low, high = low_order.index(j), high_order.index(j)
+        decay = jnp.where(late, read_decay(high_ref[high, half:]), read_decay(low_ref[low, half:]))
+        own = jnp.where(late, high_ref[high, :half].astype(F32), low_ref[low, :half].astype(F32))
+        state = jnp.where(j < place, decay * state + own, state)
     for b in range(n):
         at = order.index(b)
         o_ref[at] = state.astype(B16)
@@ -180,8 +192,9 @@
     mps = lax.axis_size("mp")
     half = heads * HEAD_DIM // members
     mac = 2 * heads * tok * HEAD_DIM * HEAD_DIM
-    z_order = [(5 * groups) // 8]
-    z_order += [z for z in range(groups)[::-1] if z not in z_order]
+    count = groups // 2
+    low_order = list(range(count))[::-1]
+    high_order = [1, *range(count)[:1:-1], 0]
     order = rotated(members, (13 * members) // 16)
     y_order = rotated(mps, mps // 2)
     gates = log_decay.T
@@ -207,11 +220,21 @@
     blocks = exchange(own, "g", order)
     total, decays = local(
         functools.partial(total_kernel, order),
-        [((groups, half + EXTRA, HEAD_DIM), B16), ((members, HEAD_DIM), F32)],
+        [((count, half + EXTRA, HEAD_DIM), B16), ((members, HEAD_DIM), F32)],
         blocks,
     )
-    totals = exchange(total, "zh", z_order)
-    place = lax.axis_index("zh").astype(jnp.int32).reshape(1)
+    zh = lax.axis_index("zh")
+    place = zh.astype(jnp.int32).reshape(1)
+    z_groups = [low_order, [count + j for j in high_order]]
+
+    def swap(a):
+        return lax.all_to_all(a, "zh", 0, 0, tiled=True, axis_index_groups=z_groups)
+
+    low = lax.cond(zh < count, swap, lambda a: a, total)
+    (sent,) = local(functools.partial(half_kernel, low_order), [((half, HEAD_DIM), B16)], low)
+    first = lax.ppermute(sent, "zh", [(j, groups - 1 - j) for j in range(count)])
+    total, sent = lax.optimization_barrier((total, sent))
+    high = lax.cond(zh < count, lambda a: a, swap, total)
     inner, grown = local(
         inner_kernel,
         [((tok, width), F32), ((tok, heads), F32)],
@@ -221,12 +244,14 @@
         gates,
         flops=2 * mac,
     )
-    totals, inner, grown = lax.optimization_barrier((totals, inner, grown))
+    high, inner, grown = lax.optimization_barrier((high, inner, grown))
     (prior,) = local(
-        functools.partial(prior_kernel, z_order, order),
+        functools.partial(prior_kernel, low_order, high_order, order),
         [((members, half, HEAD_DIM), B16)],
         place,
-        totals,
+        low,
+        high,
+        first,
         blocks,
         decays,
         spaces=(pltpu.SMEM,),

time: 60.8 us -> 56.1 us (0.923)
  starting transfers between devices: 12.1 us -> 10.1 us
  blocking collectives: 35.3 us -> 33.4 us
  local copies, waits for them, and re-layouts: 0.71 us -> 0.04 us
  Pallas kernels: 5.39 us -> 4.73 us
    all_to_all x3 -> x2, blocking collectives: 35.3 us -> 20 us  [exchange(): return lax.all_to_all(a, axis, 0, 0, tiled=True, axis_index_groups=[order])]
    all_to_all x0 -> x1, blocking collectives: none -> 13.5 us  [swap(): return lax.all_to_all(a, 'zh', 0, 0, tiled=True, axis_index_groups=z_groups)]
    all_to_all x1, starting transfers between devices: 12.1 us -> 8.77 us  [exchange(): return lax.all_to_all(a, axis, 0, 0, tiled=True, axis_index_groups=[order])]
    ppermute x0 -> x1, starting transfers between devices: none -> 1.29 us  [body(): lax.ppermute(sent, 'zh', [(j, groups - 1 - j) for j in range(count)])]
    unnamed x10, local copies, waits for them, and re-layouts: 0.69 us -> 0.03 us
    pallas_call x5 -> x6, Pallas kernels: 5.39 us -> 4.73 us  [local(): pl.pallas_call(kernel, out_shape=[jax.ShapeDtypeStruct(shape, dtype) for...]
  transfers between devices with their start and end apart: 1 -> 2, of which waited for: 1 -> 1; matrix products, arithmetic and copies ran while one was open for 0% -> 0% of each run, Pallas kernels for 2% -> 3%
where the time goes in v5:
time: 56.1 us; the launch traced here: 55.7 us
  blocking collectives  33.4 us (60%)
  starting transfers between devices  10.1 us (18%)
  waiting for transfers between devices  6.61 us (12%)
  Pallas kernels  4.73 us (8%)
  other arithmetic  0.72 us (1%)
    all_to_all x2, blocking collectives, exchange(): return lax.all_to_all(a, axis, 0, 0, tiled=True, axis_index_groups=[order])  20 us
    all_to_all x1, blocking collectives, swap(): return lax.all_to_all(a, 'zh', 0, 0, tiled=True, axis_index_groups=z_groups)  13.5 us
    all_to_all x1, starting transfers between devices, exchange(): return lax.all_to_all(a, axis, 0, 0, tiled=True, axis_index_groups=[order])  8.77 us
    all_to_all x1, waiting for transfers between devices, exchange(): return lax.all_to_all(a, axis, 0, 0, tiled=True, axis_index_groups=[order])  6.61 us
    pallas_call x6, Pallas kernels, local(): pl.pallas_call(kernel, out_shape=[jax.ShapeDtypeStruct(shape, dtype) for...  4.73 us
    ppermute x1, starting transfers between devices, body(): lax.ppermute(sent, 'zh', [(j, groups - 1 - j) for j in range(count)])  1.29 us
  transfers between devices with their start and end apart: 2, of which 1 were waited for; matrix products, arithmetic and copies ran while one was open for 0% of the time, Pallas kernels for 3%

profile of v5, /device:TPU:6, one launch (start us, length us, event | category | flops | bytes accessed | tf_op | source)
XLA Modules:
  0.0 55.7 jit_solution(4847688162455114139)
XLA Ops:
  0.0 2.3 %shard_map.55 = bf16[16,72,128]{2,1,0:T(8,128)(2,1)} custom-call(bf16[128,1024]{1,0:T(8,128)(2,1)} %k_ref.1, bf16[128,1024]{1,0:T(8,128)(2,1)} %v_ref.1, f32[8,128]{1,0:T(8,128)} %bitcast.13), custom_call_target="tpu_custom_call" | custom-call | flops 33554432 | bytes 528384 | tf_op jit(solution)/shard_map/pallas_call | solution.py:170
  2.3 0.0 copy-start.2
  2.4 8.8 %all-to-all-start.2 = ((bf16[16,72,128]{2,1,0:T(8,128)(2,1)}), bf16[16,72,128]{2,1,0:T(8,128)(2,1)S(1)}, u32[]{:S(2)}, u32[]{:S(2)}) async-start(bf16[16,72,128]{2,1,0:T(8,128)(2,1)} %shard_map.55), calls=%async_computation.2 | async-start | bytes 589824 | tf_op jit(solution)/shard_map/all_to_all | solution.py:186
  11.1 6.6 %all-to-all-done.2.x_ref = bf16[16,72,128]{2,1,0:T(8,128)(2,1)S(1)} async-done(((bf16[16,72,128]{2,1,0:T(8,128)(2,1)}), bf16[16,72,128]{2,1,0:T(8,128)(2,1)S(1)}, u32[]{:S(2)}, u32[]{:S(2)}) %all-to-all-start.2) | async-done | bytes 294944 | tf_op jit(solution)/shard_map/all_to_all | solution.py:186
  17.7 0.0 copy-start.1
  17.7 0.1 shard_map.56
  17.8 0.0 copy-start
  17.8 13.5 %conditional.2 = (bf16[4,72,128]{2,1,0:T(8,128)(2,1)S(1)}) conditional(s32[]{:T(128)} %convert_element_type.4, bf16[4,72,128]{2,1,0:T(8,128)(2,1)S(1)} %get-tuple-element.24, bf16[4,72,128]{2,1,0:T(8,128)(2,1)S(1)} %get-tuple-element.24), branch_computations={%region_0.0_spmd, %region_1.0_spmd} | conditional | bytes 147464 | solution.py:233
  17.8 13.5 %all_to_all.23 = bf16[4,72,128]{2,1,0:T(8,128)(2,1)S(1)} all-to-all(bf16[4,72,128]{2,1,0:T(8,128)(2,1)S(1)} %param.1), channel_id=1, replica_groups={{192,128,64,0},{320,448,384,256},{193,129,65,1},{321,449,385,257},{194,..., dimensions={0} | all-to-all | bytes 147456 | tf_op jit(solution)/shard_map/cond/branch_1_fun/all_to_all | solution.py:231
  31.3 0.0 copy-start.3
  31.3 1.3 %collective-permute-start = (bf16[64,128]{1,0:T(8,128)(2,1)S(1)}, bf16[64,128]{1,0:T(8,128)(2,1)S(1)}, u32[]{:S(2)}, u32[]{:S(2)}) collective-permute-start(bf16[64,128]{1,0:T(8,128)(2,1)S(1)} %shard_map.57), channel_id=1, source_target_pairs={{0,448},{64,384},{128,320},{192,256},{1,449},{65,385},{129,321},{1... | collective-permute-start | bytes 49160 | tf_op jit(solution)/shard_map/ppermute | solution.py:235
  32.6 0.0 copy-done.2
  32.6 0.0 copy-done.1
  32.6 0.0 copy-done
  32.7 0.0 copy-done.3
  32.7 1.4 %shard_map.58 = (f32[128,1024]{1,0:T(8,128)S(1)}, f32[128,8]{1,0:T(8,128)S(1)}) custom-call(bf16[128,1024]{1,0:T(8,128)(2,1)S(1)} %copy-done.2, bf16[128,1024]{1,0:T(8,128)(2,1)S(1)} %copy-done, bf16[128,1024]{1,0:T(8,128)(2,1)S(1)} %copy-done.1, f32[8,128]{1,0:T(8,128)S(1)} %bitcast.14), custom_call_target="tpu_custom_call" | custom-call | flops 67108864 | bytes 790528 | tf_op jit(solution)/shard_map/pallas_call | solution.py:170
  34.1 0.0 collective-permute-done.first_ref
  34.2 0.1 shard_map.59
  34.3 0.0 copy-start.4
  34.3 10.0 %all_to_all.25 = bf16[16,64,128]{2,1,0:T(8,128)(2,1)S(1)} all-to-all(bf16[16,64,128]{2,1,0:T(8,128)(2,1)S(1)} %shard_map.59), channel_id=1, replica_groups={{52,56,60,0,4,8,12,16,20,24,28,32,36,40,44,48},{53,57,61,1,5,9,13,17,21..., dimensions={0} | all-to-all | bytes 524288 | tf_op jit(solution)/shard_map/all_to_all | solution.py:186
  44.2 0.0 copy-done.4
  44.2 0.8 %shard_map.60 = bf16[4,32,1024]{2,1,0:T(8,128)(2,1)S(1)} custom-call(bf16[128,1024]{1,0:T(8,128)(2,1)S(1)} %copy-done.2, bf16[8,128,128]{2,1,0:T(8,128)(2,1)S(1)} %bitcast.12, f32[128,1024]{1,0:T(8,128)S(1)} %get-tuple-element.29.i_ref, f32[128,8]{1,0:T(8,128)S(1)} %get-tuple-element.30.e_ref, f32[1,1024]{1,0:T(1,128)S(1)} %bitcast.15), custom_call_target="tpu_custom_call" | custom-call | flops 33554432 | bytes 1056768 | tf_op jit(solution)/shard_map/pallas_call | solution.py:170
  45.0 10.0 %all_to_all.26 = bf16[4,32,1024]{2,1,0:T(8,128)(2,1)S(1)} all-to-all(bf16[4,32,1024]{2,1,0:T(8,128)(2,1)S(1)} %shard_map.60), channel_id=1, replica_groups={{2,3,0,1},{6,7,4,5},{10,11,8,9},{14,15,12,13},{18,19,16,17},{22,23,20,2..., dimensions={0} | all-to-all | bytes 524288 | tf_op jit(solution)/shard_map/all_to_all | solution.py:186
  55.0 0.7 %pad_maximum_fusion = bf16[32,4096]{1,0:T(8,128)(2,1)} fusion(bf16[32,1024]{1,0:T(8,128)(2,1)S(1)} %get-tuple-element.32, bf16[32,1024]{1,0:T(8,128)(2,1)S(1)} %get-tuple-element.33, bf16[32,1024]{1,0:T(8,128)(2,1)S(1)} %get-tuple-element.34, bf16[32,1024]{1,0:T(8,128)(2,1)S(1)} %get-tuple-element.31), kind=kLoop, calls=%fused_computation | loop fusion | flops 1048576 | bytes 524288 | tf_op jit(solution)/shard_map/concatenate | solution.py:271
  (3 shorter events, 0.1 us)
Async XLA Ops:
  2.3 30.3 %copy-start.2 = (bf16[128,1024]{1,0:T(8,128)(2,1)S(1)}, bf16[128,1024]{1,0:T(8,128)(2,1)}, u32[]{:S(2)}) copy-start(bf16[128,1024]{1,0:T(8,128)(2,1)} %q_ref.3) | copy-start | bytes 786436
  2.4 15.4 %all-to-all-start.2 = ((bf16[16,72,128]{2,1,0:T(8,128)(2,1)}), bf16[16,72,128]{2,1,0:T(8,128)(2,1)S(1)}, u32[]{:S(2)}, u32[]{:S(2)}) async-start(bf16[16,72,128]{2,1,0:T(8,128)(2,1)} %shard_map.55), calls=%async_computation.2 | async-start | bytes 589824 | tf_op jit(solution)/shard_map/all_to_all | solution.py:186
  17.7 14.9 %copy-start.1 = (bf16[128,1024]{1,0:T(8,128)(2,1)S(1)}, bf16[128,1024]{1,0:T(8,128)(2,1)}, u32[]{:S(2)}) copy-start(bf16[128,1024]{1,0:T(8,128)(2,1)} %v_ref.1) | copy-start | bytes 786436
  17.8 14.8 %copy-start = (bf16[128,1024]{1,0:T(8,128)(2,1)S(1)}, bf16[128,1024]{1,0:T(8,128)(2,1)}, u32[]{:S(2)}) copy-start(bf16[128,1024]{1,0:T(8,128)(2,1)} %k_ref.1) | copy-start | bytes 786436
  31.3 1.4 %copy-start.3 = (f32[128,8]{0,1:T(8,128)S(1)}, f32[128,8]{0,1:T(8,128)}, u32[]{:S(2)}) copy-start(f32[128,8]{0,1:T(8,128)} %param.12) | copy-start | bytes 12292
  31.3 2.8 %collective-permute-start = (bf16[64,128]{1,0:T(8,128)(2,1)S(1)}, bf16[64,128]{1,0:T(8,128)(2,1)S(1)}, u32[]{:S(2)}, u32[]{:S(2)}) collective-permute-start(bf16[64,128]{1,0:T(8,128)(2,1)S(1)} %shard_map.57), channel_id=1, source_target_pairs={{0,448},{64,384},{128,320},{192,256},{1,449},{65,385},{129,321},{1... | collective-permute-start | bytes 49160 | tf_op jit(solution)/shard_map/ppermute | solution.py:235
  34.3 10.0 %copy-start.4 = (f32[1024]{0:T(1024)S(1)}, f32[1024]{0:T(1024)}, u32[]{:S(2)}) copy-start(f32[1024]{0:T(1024)} %param.13) | copy-start | bytes 12292

commit v6 on v4

--- a/solution.py
+++ b/solution.py
@@ -89,7 +89,8 @@
         copy.wait()
 
 
-def total_kernel(order, x_ref, o_ref, d_ref):
+def total_kernel(order, x_ref, *refs):
+    *o_refs, d_ref = refs
     n, rows, _ = x_ref.shape
     half = rows - EXTRA
     for b in range(n):
@@ -101,19 +102,39 @@
         decay = decay * d if b else d
     state = state.astype(B16)
     tail = decay_rows(decay)
-    for j in range(o_ref.shape[0]):
-        o_ref[j, :half] = state
-        o_ref[j, half:] = tail
-
-
-def prior_kernel(z_order, order, place_ref, z_ref, x_ref, d_ref, o_ref):
-    place = place_ref[0]
+    for o_ref in o_refs:
+        for j in range(o_ref.shape[0]):
+            o_ref[j, :half] = state
+            o_ref[j, half:] = tail
+
+
+def sum_kernel(order, *refs):
+    *first, z_ref, o_ref = refs
+    half = o_ref.shape[0]
+    state = first[0][...].astype(F32) if first else jnp.zeros((half, HEAD_DIM), F32)
+    for j in range(z_ref.shape[0]):
+        at = order.index(j)
+        state = read_decay(z_ref[at, half:]) * state + z_ref[at, :half].astype(F32)
+    o_ref[...] = state.astype(B16)
+
+
+def prior_kernel(pair, four, order, place_ref, z0_ref, z1_ref, z2_ref, p1_ref, pa_ref, pb_ref, x_ref, d_ref, o_ref):
     n, half, _ = o_ref.shape
-    state = jnp.zeros((half, HEAD_DIM), F32)
-    for j in range(z_ref.shape[0] - 1):
-        at = z_order.index(j)
-        later = read_decay(z_ref[at, half:]) * state + z_ref[at, :half].astype(F32)
-        state = jnp.where(j < place, later, state)
+    zh = place_ref[0]
+    second, late = zh >= 2, zh >= 4
+    by_a = (zh == 5) | (zh == 6)
+    place = jnp.where(late, zh - 4, jnp.where(second, zh - 2, zh))
+    came = jnp.where(by_a, pa_ref[...].astype(F32), pb_ref[...].astype(F32))
+    state = jnp.where(late, came, jnp.where(second, p1_ref[...].astype(F32), 0.0))
+    for j in range(len(four) - 1):
+        at = four.index(j)
+        decay, own = read_decay(z2_ref[at, half:]), z2_ref[at, :half].astype(F32)
+        if j == 0:
+            at = pair.index(j)
+            for ref, take in ((z1_ref, late), (z0_ref, second)):
+                decay_e, own_e = read_decay(ref[at, half:]), ref[at, :half].astype(F32)
+                decay, own = jnp.where(take, decay, decay_e), jnp.where(take, own, own_e)
+        state = jnp.where(j < place, decay * state + own, state)
     for b in range(n):
         at = order.index(b)
         o_ref[at] = state.astype(B16)
@@ -180,8 +201,8 @@
     mps = lax.axis_size("mp")
     half = heads * HEAD_DIM // members
     mac = 2 * heads * tok * HEAD_DIM * HEAD_DIM
-    z_order = [(5 * groups) // 8]
-    z_order += [z for z in range(groups)[::-1] if z not in z_order]
+    assert groups == 8
+    pair, four = [1, 0], [1, 3, 2, 0]
     order = rotated(members, (13 * members) // 16)
     y_order = rotated(mps, mps // 2)
     gates = log_decay.T
@@ -205,13 +226,6 @@
         vmem=60,
     )
     blocks = exchange(own, "g", order)
-    total, decays = local(
-        functools.partial(total_kernel, order),
-        [((groups, half + EXTRA, HEAD_DIM), B16), ((members, HEAD_DIM), F32)],
-        blocks,
-    )
-    totals = exchange(total, "zh", z_order)
-    place = lax.axis_index("zh").astype(jnp.int32).reshape(1)
     inner, grown = local(
         inner_kernel,
         [((tok, width), F32), ((tok, heads), F32)],
@@ -221,12 +235,47 @@
         gates,
         flops=2 * mac,
     )
-    totals, inner, grown = lax.optimization_barrier((totals, inner, grown))
+    blocks, inner, grown = lax.optimization_barrier((blocks, inner, grown))
+    rows = half + EXTRA
+    total2, total4, decays = local(
+        functools.partial(total_kernel, order),
+        [((2, rows, HEAD_DIM), B16), ((4, rows, HEAD_DIM), B16), ((members, HEAD_DIM), F32)],
+        blocks,
+    )
+    zh = lax.axis_index("zh")
+    place = zh.astype(jnp.int32).reshape(1)
+
+    def among(group):
+        n = len(group)
+        lists = [[first + j for j in group] for first in range(0, groups, n)]
+        return lambda a: lax.all_to_all(a, "zh", 0, 0, tiled=True, axis_index_groups=lists)
+
+    def same(a):
+        return a
+
+    def added(*args):
+        return local(functools.partial(sum_kernel, pair), [((half, HEAD_DIM), B16)], *args)[0]
+
+    z0 = lax.cond(zh < 2, among(pair), same, total2)
+    sum0 = added(z0)
+    first = lax.ppermute(sum0, "zh", [(0, 2), (1, 3)])
+    total2, sum0 = lax.optimization_barrier((total2, sum0))
+    z1 = lax.cond((zh >= 2) & (zh < 4), among(pair), same, total2)
+    sum1 = added(first, z1)
+    came_a = lax.ppermute(sum1, "zh", [(3, 5), (2, 6)])
+    came_b = lax.ppermute(sum1, "zh", [(3, 4), (2, 7)])
+    total4, sum1 = lax.optimization_barrier((total4, sum1))
+    z2 = lax.cond(zh >= 4, among(four), same, total4)
     (prior,) = local(
-        functools.partial(prior_kernel, z_order, order),
+        functools.partial(prior_kernel, pair, four, order),
         [((members, half, HEAD_DIM), B16)],
         place,
-        totals,
+        z0,
+        z1,
+        z2,
+        first,
+        came_a,
+        came_b,
         blocks,
         decays,
         spaces=(pltpu.SMEM,),

time: 60.8 us -> 53 us (0.87)
  the two profiles are of different devices: /device:TPU:6 before, /device:TPU:422 now
where the time goes in v6:
time: 53 us; the launch traced here: 52.6 us
  blocking collectives  30.1 us (57%)
  waiting for transfers between devices  9.77 us (18%)
  starting transfers between devices  6.35 us (12%)
  Pallas kernels  4.77 us (9%)
  other arithmetic  0.72 us (1%)
  local copies, waits for them, and re-layouts  0.7 us (1%)
    all_to_all x2, blocking collectives, exchange(): return lax.all_to_all(a, axis, 0, 0, tiled=True, axis_index_groups=[order])  18.7 us
    all_to_all x1, blocking collectives, among(): lax.all_to_all(a, 'zh', 0, 0, tiled=True, axis_index_groups=lists)  11.4 us
    all_to_all x1, waiting for transfers between devices, exchange(): return lax.all_to_all(a, axis, 0, 0, tiled=True, axis_index_groups=[order])  5.37 us
    pallas_call x7, Pallas kernels, local(): pl.pallas_call(kernel, out_shape=[jax.ShapeDtypeStruct(shape, dtype) for...  4.77 us
    ppermute x1, waiting for transfers between devices, body(): came_a = lax.ppermute(sum1, 'zh', [(3, 5), (2, 6)])  4.39 us
    all_to_all x1, starting transfers between devices, exchange(): return lax.all_to_all(a, axis, 0, 0, tiled=True, axis_index_groups=[order])  3.73 us
    ppermute x1, starting transfers between devices, body(): came_a = lax.ppermute(sum1, 'zh', [(3, 5), (2, 6)])  1.29 us
  transfers between devices with their start and end apart: 4, of which 2 were waited for; matrix products, arithmetic and copies ran while one was open for 0% of the time, Pallas kernels for 3%

profile of v6, /device:TPU:422, one launch (start us, length us, event | category | flops | bytes accessed | tf_op | source)
XLA Modules:
  0.0 52.6 jit_solution(16590817384419080856)
XLA Ops:
  0.0 0.0 copy-start.2
  0.0 2.4 %shard_map.55 = bf16[16,72,128]{2,1,0:T(8,128)(2,1)} custom-call(bf16[128,1024]{1,0:T(8,128)(2,1)} %k_ref.1, bf16[128,1024]{1,0:T(8,128)(2,1)} %v_ref.1, f32[8,128]{1,0:T(8,128)} %bitcast.13), custom_call_target="tpu_custom_call" | custom-call | flops 33554432 | bytes 528384 | tf_op jit(solution)/shard_map/pallas_call | solution.py:179
  2.4 0.0 copy-start
  2.4 0.0 copy-start.1
  2.4 3.7 %all-to-all-start.3 = ((bf16[16,72,128]{2,1,0:T(8,128)(2,1)}), bf16[16,72,128]{2,1,0:T(8,128)(2,1)S(1)}, u32[]{:S(2)}, u32[]{:S(2)}) async-start(bf16[16,72,128]{2,1,0:T(8,128)(2,1)} %shard_map.55), calls=%async_computation.3 | async-start | bytes 589824 | tf_op jit(solution)/shard_map/all_to_all | solution.py:195
  6.1 0.0 copy-start.3
  6.2 0.0 copy-done.2
  6.2 0.0 copy-done
  6.2 0.0 copy-done.1
  6.2 0.6 %copy-done.3 = f32[128,8]{0,1:T(8,128)S(1)} copy-done((f32[128,8]{0,1:T(8,128)S(1)}, f32[128,8]{0,1:T(8,128)}, u32[]{:S(2)}) %copy-start.3) | copy-done | bytes 4120
  6.8 1.4 %shard_map.56 = (f32[128,1024]{1,0:T(8,128)S(1)}, f32[128,8]{1,0:T(8,128)S(1)}) custom-call(bf16[128,1024]{1,0:T(8,128)(2,1)S(1)} %copy-done.2, bf16[128,1024]{1,0:T(8,128)(2,1)S(1)} %copy-done, bf16[128,1024]{1,0:T(8,128)(2,1)S(1)} %copy-done.1, f32[8,128]{1,0:T(8,128)S(1)} %bitcast.14), custom_call_target="tpu_custom_call" | custom-call | flops 67108864 | bytes 790528 | tf_op jit(solution)/shard_map/pallas_call | solution.py:179
  8.3 5.4 %all-to-all-done.3.x_ref = bf16[16,72,128]{2,1,0:T(8,128)(2,1)S(1)} async-done(((bf16[16,72,128]{2,1,0:T(8,128)(2,1)}), bf16[16,72,128]{2,1,0:T(8,128)(2,1)S(1)}, u32[]{:S(2)}, u32[]{:S(2)}) %all-to-all-start.3) | async-done | bytes 294944 | tf_op jit(solution)/shard_map/all_to_all | solution.py:195
  13.7 0.1 shard_map.57
  13.8 0.7 %collective-permute-start = (bf16[64,128]{1,0:T(8,128)(2,1)S(1)}, bf16[64,128]{1,0:T(8,128)(2,1)S(1)}, u32[]{:S(2)}, u32[]{:S(2)}) collective-permute-start(bf16[64,128]{1,0:T(8,128)(2,1)S(1)} %shard_map.58), channel_id=1, source_target_pairs={{0,128},{64,192},{1,129},{65,193},{2,130},{66,194},{3,131},{67,195... | collective-permute-start | bytes 49160 | tf_op jit(solution)/shard_map/ppermute | solution.py:261
  14.5 0.0 collective-permute-done.refs_0_.p1_ref
  14.5 0.7 %collective-permute-start.2 = (bf16[64,128]{1,0:T(8,128)(2,1)S(1)}, bf16[64,128]{1,0:T(8,128)(2,1)S(1)}, u32[]{:S(2)}, u32[]{:S(2)}) collective-permute-start(bf16[64,128]{1,0:T(8,128)(2,1)S(1)} %shard_map.59), channel_id=1, source_target_pairs={{192,256},{128,448},{193,257},{129,449},{194,258},{130,450},{195,2... | collective-permute-start | bytes 49160 | tf_op jit(solution)/shard_map/ppermute | solution.py:266
  15.2 1.3 %collective-permute-start.1 = (bf16[64,128]{1,0:T(8,128)(2,1)S(1)}, bf16[64,128]{1,0:T(8,128)(2,1)S(1)}, u32[]{:S(2)}, u32[]{:S(2)}) collective-permute-start(bf16[64,128]{1,0:T(8,128)(2,1)S(1)} %shard_map.59), channel_id=1, source_target_pairs={{192,320},{128,384},{193,321},{129,385},{194,322},{130,386},{195,3... | collective-permute-start | bytes 49160 | tf_op jit(solution)/shard_map/ppermute | solution.py:265
  16.5 11.4 %conditional.5 = (bf16[4,72,128]{2,1,0:T(8,128)(2,1)S(1)}) conditional(s32[]{:T(128)} %convert_element_type.11, bf16[4,72,128]{2,1,0:T(8,128)(2,1)S(1)} %get-tuple-element.36, bf16[4,72,128]{2,1,0:T(8,128)(2,1)S(1)} %get-tuple-element.36), branch_computations={%region_4.0_spmd, %region_5.0_spmd} | conditional | bytes 294920 | solution.py:268
  16.5 11.4 %all_to_all.29 = bf16[4,72,128]{2,1,0:T(8,128)(2,1)S(1)} all-to-all(bf16[4,72,128]{2,1,0:T(8,128)(2,1)S(1)} %copy.13), channel_id=1, replica_groups={{64,192,128,0},{320,448,384,256},{65,193,129,1},{321,449,385,257},{66,1..., dimensions={0} | all-to-all | bytes 147456 | tf_op jit(solution)/shard_map/cond/branch_1_fun/all_to_all | solution.py:251
  27.9 0.0 collective-permute-done.2.pb_ref
  27.9 4.4 %collective-permute-done.1.pa_ref = bf16[64,128]{1,0:T(8,128)(2,1)S(1)} collective-permute-done((bf16[64,128]{1,0:T(8,128)(2,1)S(1)}, bf16[64,128]{1,0:T(8,128)(2,1)S(1)}, u32[]{:S(2)}, u32[]{:S(2)}) %collective-permute-start.1) | collective-permute-done | bytes 16416 | tf_op jit(solution)/shard_map/ppermute | solution.py:265
  32.3 0.1 shard_map.60
  32.4 0.0 copy-start.4
  32.4 10.0 %all_to_all.30 = bf16[16,64,128]{2,1,0:T(8,128)(2,1)S(1)} all-to-all(bf16[16,64,128]{2,1,0:T(8,128)(2,1)S(1)} %shard_map.60), channel_id=1, replica_groups={{52,56,60,0,4,8,12,16,20,24,28,32,36,40,44,48},{53,57,61,1,5,9,13,17,21..., dimensions={0} | all-to-all | bytes 524288 | tf_op jit(solution)/shard_map/all_to_all | solution.py:195
  42.4 0.0 copy-done.4
  42.4 0.8 %shard_map.61 = bf16[4,32,1024]{2,1,0:T(8,128)(2,1)S(1)} custom-call(bf16[128,1024]{1,0:T(8,128)(2,1)S(1)} %copy-done.2, bf16[8,128,128]{2,1,0:T(8,128)(2,1)S(1)} %bitcast.12, f32[128,1024]{1,0:T(8,128)S(1)} %get-tuple-element.38.i_ref, f32[128,8]{1,0:T(8,128)S(1)} %get-tuple-element.39.e_ref, f32[1,1024]{1,0:T(1,128)S(1)} %bitcast.15), custom_call_target="tpu_custom_call" | custom-call | flops 33554432 | bytes 1056768 | tf_op jit(solution)/shard_map/pallas_call | solution.py:179
  43.1 8.7 %all_to_all.31 = bf16[4,32,1024]{2,1,0:T(8,128)(2,1)S(1)} all-to-all(bf16[4,32,1024]{2,1,0:T(8,128)(2,1)S(1)} %shard_map.61), channel_id=1, replica_groups={{2,3,0,1},{6,7,4,5},{10,11,8,9},{14,15,12,13},{18,19,16,17},{22,23,20,2..., dimensions={0} | all-to-all | bytes 524288 | tf_op jit(solution)/shard_map/all_to_all | solution.py:195
  51.9 0.7 %pad_maximum_fusion = bf16[32,4096]{1,0:T(8,128)(2,1)} fusion(bf16[32,1024]{1,0:T(8,128)(2,1)S(1)} %get-tuple-element.41, bf16[32,1024]{1,0:T(8,128)(2,1)S(1)} %get-tuple-element.42, bf16[32,1024]{1,0:T(8,128)(2,1)S(1)} %get-tuple-element.43, bf16[32,1024]{1,0:T(8,128)(2,1)S(1)} %get-tuple-element.40), kind=kLoop, calls=%fused_computation | loop fusion | flops 1048576 | bytes 524288 | tf_op jit(solution)/shard_map/concatenate | solution.py:295
  (7 shorter events, 0.1 us)
Async XLA Ops:
  0.0 6.2 %copy-start.2 = (bf16[128,1024]{1,0:T(8,128)(2,1)S(1)}, bf16[128,1024]{1,0:T(8,128)(2,1)}, u32[]{:S(2)}) copy-start(bf16[128,1024]{1,0:T(8,128)(2,1)} %q_ref.3) | copy-start | bytes 786436
  2.4 3.8 %copy-start = (bf16[128,1024]{1,0:T(8,128)(2,1)S(1)}, bf16[128,1024]{1,0:T(8,128)(2,1)}, u32[]{:S(2)}) copy-start(bf16[128,1024]{1,0:T(8,128)(2,1)} %k_ref.1) | copy-start | bytes 786436
  2.4 3.8 %copy-start.1 = (bf16[128,1024]{1,0:T(8,128)(2,1)S(1)}, bf16[128,1024]{1,0:T(8,128)(2,1)}, u32[]{:S(2)}) copy-start(bf16[128,1024]{1,0:T(8,128)(2,1)} %v_ref.1) | copy-start | bytes 786436
  2.4 11.2 %all-to-all-start.3 = ((bf16[16,72,128]{2,1,0:T(8,128)(2,1)}), bf16[16,72,128]{2,1,0:T(8,128)(2,1)S(1)}, u32[]{:S(2)}, u32[]{:S(2)}) async-start(bf16[16,72,128]{2,1,0:T(8,128)(2,1)} %shard_map.55), calls=%async_computation.3 | async-start | bytes 589824 | tf_op jit(solution)/shard_map/all_to_all | solution.py:195
  6.1 0.7 %copy-start.3 = (f32[128,8]{0,1:T(8,128)S(1)}, f32[128,8]{0,1:T(8,128)}, u32[]{:S(2)}) copy-start(f32[128,8]{0,1:T(8,128)} %param.14) | copy-start | bytes 12292
  13.8 0.7 %collective-permute-start = (bf16[64,128]{1,0:T(8,128)(2,1)S(1)}, bf16[64,128]{1,0:T(8,128)(2,1)S(1)}, u32[]{:S(2)}, u32[]{:S(2)}) collective-permute-start(bf16[64,128]{1,0:T(8,128)(2,1)S(1)} %shard_map.58), channel_id=1, source_target_pairs={{0,128},{64,192},{1,129},{65,193},{2,130},{66,194},{3,131},{67,195... | collective-permute-start | bytes 49160 | tf_op jit(solution)/shard_map/ppermute | solution.py:261
  14.5 13.4 %collective-permute-start.2 = (bf16[64,128]{1,0:T(8,128)(2,1)S(1)}, bf16[64,128]{1,0:T(8,128)(2,1)S(1)}, u32[]{:S(2)}, u32[]{:S(2)}) collective-permute-start(bf16[64,128]{1,0:T(8,128)(2,1)S(1)} %shard_map.59), channel_id=1, source_target_pairs={{192,256},{128,448},{193,257},{129,449},{194,258},{130,450},{195,2... | collective-permute-start | bytes 49160 | tf_op jit(solution)/shard_map/ppermute | solution.py:266
  15.2 17.1 %collective-permute-start.1 = (bf16[64,128]{1,0:T(8,128)(2,1)S(1)}, bf16[64,128]{1,0:T(8,128)(2,1)S(1)}, u32[]{:S(2)}, u32[]{:S(2)}) collective-permute-start(bf16[64,128]{1,0:T(8,128)(2,1)S(1)} %shard_map.59), channel_id=1, source_target_pairs={{192,320},{128,384},{193,321},{129,385},{194,322},{130,386},{195,3... | collective-permute-start | bytes 49160 | tf_op jit(solution)/shard_map/ppermute | solution.py:265
  32.4 10.0 %copy-start.4 = (f32[1024]{0:T(1024)S(1)}, f32[1024]{0:T(1024)}, u32[]{:S(2)}) copy-start(f32[1024]{0:T(1024)} %param.15) | copy-start | bytes 12292

commit v7 on v6

--- a/solution.py
+++ b/solution.py
@@ -122,7 +122,7 @@
     n, half, _ = o_ref.shape
     zh = place_ref[0]
     second, late = zh >= 2, zh >= 4
-    by_a = (zh == 5) | (zh == 6)
+    by_a = (zh == 4) | (zh == 7)
     place = jnp.where(late, zh - 4, jnp.where(second, zh - 2, zh))
     came = jnp.where(by_a, pa_ref[...].astype(F32), pb_ref[...].astype(F32))
     state = jnp.where(late, came, jnp.where(second, p1_ref[...].astype(F32), 0.0))
@@ -262,8 +262,8 @@
     total2, sum0 = lax.optimization_barrier((total2, sum0))
     z1 = lax.cond((zh >= 2) & (zh < 4), among(pair), same, total2)
     sum1 = added(first, z1)
-    came_a = lax.ppermute(sum1, "zh", [(3, 5), (2, 6)])
-    came_b = lax.ppermute(sum1, "zh", [(3, 4), (2, 7)])
+    came_a = lax.ppermute(sum1, "zh", [(3, 4), (2, 7)])
+    came_b = lax.ppermute(sum1, "zh", [(3, 6), (2, 5)])
     total4, sum1 = lax.optimization_barrier((total4, sum1))
     z2 = lax.cond(zh >= 4, among(four), same, total4)
     (prior,) = local(

time: 53 us -> 52.3 us (0.987)
  waiting for transfers between devices: 9.77 us -> 9.06 us
    ppermute x2, waiting for transfers between devices: 4.39 us -> 3.68 us  [the longest x1 3.68 us: body(): came_b = lax.ppermute(sum1, 'zh', [(3, 6), (2, 5)])]
where the time goes in v7:
time: 52.3 us; the launch traced here: 51.9 us
  blocking collectives  30.1 us (58%)
  waiting for transfers between devices  9.06 us (17%)
  starting transfers between devices  6.35 us (12%)
  Pallas kernels  4.77 us (9%)
  other arithmetic  0.72 us (1%)
  local copies, waits for them, and re-layouts  0.7 us (1%)
    all_to_all x2, blocking collectives, exchange(): return lax.all_to_all(a, axis, 0, 0, tiled=True, axis_index_groups=[order])  18.7 us
    all_to_all x1, blocking collectives, among(): lax.all_to_all(a, 'zh', 0, 0, tiled=True, axis_index_groups=lists)  11.4 us
    all_to_all x1, waiting for transfers between devices, exchange(): return lax.all_to_all(a, axis, 0, 0, tiled=True, axis_index_groups=[order])  5.37 us
    pallas_call x7, Pallas kernels, local(): pl.pallas_call(kernel, out_shape=[jax.ShapeDtypeStruct(shape, dtype) for...  4.77 us
    all_to_all x1, starting transfers between devices, exchange(): return lax.all_to_all(a, axis, 0, 0, tiled=True, axis_index_groups=[order])  3.73 us
    ppermute x1, waiting for transfers between devices, body(): came_b = lax.ppermute(sum1, 'zh', [(3, 6), (2, 5)])  3.68 us
    ppermute x1, starting transfers between devices, body(): came_b = lax.ppermute(sum1, 'zh', [(3, 6), (2, 5)])  1.29 us
  transfers between devices with their start and end apart: 4, of which 2 were waited for; matrix products, arithmetic and copies ran while one was open for 0% of the time, Pallas kernels for 3%

profile of v7, /device:TPU:422, one launch (start us, length us, event | category | flops | bytes accessed | tf_op | source)
XLA Modules:
  0.0 51.9 jit_solution(3967435608985294180)
XLA Ops:
  0.0 0.0 copy-start.2
  0.0 2.4 %shard_map.55 = bf16[16,72,128]{2,1,0:T(8,128)(2,1)} custom-call(bf16[128,1024]{1,0:T(8,128)(2,1)} %k_ref.1, bf16[128,1024]{1,0:T(8,128)(2,1)} %v_ref.1, f32[8,128]{1,0:T(8,128)} %bitcast.13), custom_call_target="tpu_custom_call" | custom-call | flops 33554432 | bytes 528384 | tf_op jit(solution)/shard_map/pallas_call | solution.py:179
  2.4 0.0 copy-start
  2.4 0.0 copy-start.1
  2.4 3.7 %all-to-all-start.3 = ((bf16[16,72,128]{2,1,0:T(8,128)(2,1)}), bf16[16,72,128]{2,1,0:T(8,128)(2,1)S(1)}, u32[]{:S(2)}, u32[]{:S(2)}) async-start(bf16[16,72,128]{2,1,0:T(8,128)(2,1)} %shard_map.55), calls=%async_computation.3 | async-start | bytes 589824 | tf_op jit(solution)/shard_map/all_to_all | solution.py:195
  6.1 0.0 copy-start.3
  6.2 0.0 copy-done.2
  6.2 0.0 copy-done
  6.2 0.0 copy-done.1
  6.2 0.6 %copy-done.3 = f32[128,8]{0,1:T(8,128)S(1)} copy-done((f32[128,8]{0,1:T(8,128)S(1)}, f32[128,8]{0,1:T(8,128)}, u32[]{:S(2)}) %copy-start.3) | copy-done | bytes 4120
  6.8 1.4 %shard_map.56 = (f32[128,1024]{1,0:T(8,128)S(1)}, f32[128,8]{1,0:T(8,128)S(1)}) custom-call(bf16[128,1024]{1,0:T(8,128)(2,1)S(1)} %copy-done.2, bf16[128,1024]{1,0:T(8,128)(2,1)S(1)} %copy-done, bf16[128,1024]{1,0:T(8,128)(2,1)S(1)} %copy-done.1, f32[8,128]{1,0:T(8,128)S(1)} %bitcast.14), custom_call_target="tpu_custom_call" | custom-call | flops 67108864 | bytes 790528 | tf_op jit(solution)/shard_map/pallas_call | solution.py:179
  8.3 5.4 %all-to-all-done.3.x_ref = bf16[16,72,128]{2,1,0:T(8,128)(2,1)S(1)} async-done(((bf16[16,72,128]{2,1,0:T(8,128)(2,1)}), bf16[16,72,128]{2,1,0:T(8,128)(2,1)S(1)}, u32[]{:S(2)}, u32[]{:S(2)}) %all-to-all-start.3) | async-done | bytes 294944 | tf_op jit(solution)/shard_map/all_to_all | solution.py:195
  13.7 0.1 shard_map.57
  13.8 0.7 %collective-permute-start = (bf16[64,128]{1,0:T(8,128)(2,1)S(1)}, bf16[64,128]{1,0:T(8,128)(2,1)S(1)}, u32[]{:S(2)}, u32[]{:S(2)}) collective-permute-start(bf16[64,128]{1,0:T(8,128)(2,1)S(1)} %shard_map.58), channel_id=1, source_target_pairs={{0,128},{64,192},{1,129},{65,193},{2,130},{66,194},{3,131},{67,195... | collective-permute-start | bytes 49160 | tf_op jit(solution)/shard_map/ppermute | solution.py:261
  14.5 0.0 collective-permute-done.refs_0_.p1_ref
  14.5 1.3 %collective-permute-start.2 = (bf16[64,128]{1,0:T(8,128)(2,1)S(1)}, bf16[64,128]{1,0:T(8,128)(2,1)S(1)}, u32[]{:S(2)}, u32[]{:S(2)}) collective-permute-start(bf16[64,128]{1,0:T(8,128)(2,1)S(1)} %shard_map.59), channel_id=1, source_target_pairs={{192,384},{128,320},{193,385},{129,321},{194,386},{130,322},{195,3... | collective-permute-start | bytes 49160 | tf_op jit(solution)/shard_map/ppermute | solution.py:266
  15.8 0.7 %collective-permute-start.1 = (bf16[64,128]{1,0:T(8,128)(2,1)S(1)}, bf16[64,128]{1,0:T(8,128)(2,1)S(1)}, u32[]{:S(2)}, u32[]{:S(2)}) collective-permute-start(bf16[64,128]{1,0:T(8,128)(2,1)S(1)} %shard_map.59), channel_id=1, source_target_pairs={{192,256},{128,448},{193,257},{129,449},{194,258},{130,450},{195,2... | collective-permute-start | bytes 49160 | tf_op jit(solution)/shard_map/ppermute | solution.py:265
  16.5 11.4 %conditional.5 = (bf16[4,72,128]{2,1,0:T(8,128)(2,1)S(1)}) conditional(s32[]{:T(128)} %convert_element_type.11, bf16[4,72,128]{2,1,0:T(8,128)(2,1)S(1)} %get-tuple-element.36, bf16[4,72,128]{2,1,0:T(8,128)(2,1)S(1)} %get-tuple-element.36), branch_computations={%region_4.0_spmd, %region_5.0_spmd} | conditional | bytes 294920 | solution.py:268
  16.5 11.4 %all_to_all.29 = bf16[4,72,128]{2,1,0:T(8,128)(2,1)S(1)} all-to-all(bf16[4,72,128]{2,1,0:T(8,128)(2,1)S(1)} %copy.13), channel_id=1, replica_groups={{64,192,128,0},{320,448,384,256},{65,193,129,1},{321,449,385,257},{66,1..., dimensions={0} | all-to-all | bytes 147456 | tf_op jit(solution)/shard_map/cond/branch_1_fun/all_to_all | solution.py:251
  27.9 3.7 %collective-permute-done.2.pb_ref = bf16[64,128]{1,0:T(8,128)(2,1)S(1)} collective-permute-done((bf16[64,128]{1,0:T(8,128)(2,1)S(1)}, bf16[64,128]{1,0:T(8,128)(2,1)S(1)}, u32[]{:S(2)}, u32[]{:S(2)}) %collective-permute-start.2) | collective-permute-done | bytes 16416 | tf_op jit(solution)/shard_map/ppermute | solution.py:266
  31.6 0.0 collective-permute-done.1.pa_ref
  31.6 0.1 shard_map.60
  31.7 0.0 copy-start.4
  31.7 10.0 %all_to_all.30 = bf16[16,64,128]{2,1,0:T(8,128)(2,1)S(1)} all-to-all(bf16[16,64,128]{2,1,0:T(8,128)(2,1)S(1)} %shard_map.60), channel_id=1, replica_groups={{52,56,60,0,4,8,12,16,20,24,28,32,36,40,44,48},{53,57,61,1,5,9,13,17,21..., dimensions={0} | all-to-all | bytes 524288 | tf_op jit(solution)/shard_map/all_to_all | solution.py:195
  41.7 0.0 copy-done.4
  41.7 0.8 %shard_map.61 = bf16[4,32,1024]{2,1,0:T(8,128)(2,1)S(1)} custom-call(bf16[128,1024]{1,0:T(8,128)(2,1)S(1)} %copy-done.2, bf16[8,128,128]{2,1,0:T(8,128)(2,1)S(1)} %bitcast.12, f32[128,1024]{1,0:T(8,128)S(1)} %get-tuple-element.38.i_ref, f32[128,8]{1,0:T(8,128)S(1)} %get-tuple-element.39.e_ref, f32[1,1024]{1,0:T(1,128)S(1)} %bitcast.15), custom_call_target="tpu_custom_call" | custom-call | flops 33554432 | bytes 1056768 | tf_op jit(solution)/shard_map/pallas_call | solution.py:179
  42.4 8.7 %all_to_all.31 = bf16[4,32,1024]{2,1,0:T(8,128)(2,1)S(1)} all-to-all(bf16[4,32,1024]{2,1,0:T(8,128)(2,1)S(1)} %shard_map.61), channel_id=1, replica_groups={{2,3,0,1},{6,7,4,5},{10,11,8,9},{14,15,12,13},{18,19,16,17},{22,23,20,2..., dimensions={0} | all-to-all | bytes 524288 | tf_op jit(solution)/shard_map/all_to_all | solution.py:195
  51.2 0.7 %pad_maximum_fusion = bf16[32,4096]{1,0:T(8,128)(2,1)} fusion(bf16[32,1024]{1,0:T(8,128)(2,1)S(1)} %get-tuple-element.41, bf16[32,1024]{1,0:T(8,128)(2,1)S(1)} %get-tuple-element.42, bf16[32,1024]{1,0:T(8,128)(2,1)S(1)} %get-tuple-element.43, bf16[32,1024]{1,0:T(8,128)(2,1)S(1)} %get-tuple-element.40), kind=kLoop, calls=%fused_computation | loop fusion | flops 1048576 | bytes 524288 | tf_op jit(solution)/shard_map/concatenate | solution.py:295
  (7 shorter events, 0.1 us)
Async XLA Ops:
  0.0 6.2 %copy-start.2 = (bf16[128,1024]{1,0:T(8,128)(2,1)S(1)}, bf16[128,1024]{1,0:T(8,128)(2,1)}, u32[]{:S(2)}) copy-start(bf16[128,1024]{1,0:T(8,128)(2,1)} %q_ref.3) | copy-start | bytes 786436
  2.4 3.8 %copy-start = (bf16[128,1024]{1,0:T(8,128)(2,1)S(1)}, bf16[128,1024]{1,0:T(8,128)(2,1)}, u32[]{:S(2)}) copy-start(bf16[128,1024]{1,0:T(8,128)(2,1)} %k_ref.1) | copy-start | bytes 786436
  2.4 3.8 %copy-start.1 = (bf16[128,1024]{1,0:T(8,128)(2,1)S(1)}, bf16[128,1024]{1,0:T(8,128)(2,1)}, u32[]{:S(2)}) copy-start(bf16[128,1024]{1,0:T(8,128)(2,1)} %v_ref.1) | copy-start | bytes 786436
  2.4 11.2 %all-to-all-start.3 = ((bf16[16,72,128]{2,1,0:T(8,128)(2,1)}), bf16[16,72,128]{2,1,0:T(8,128)(2,1)S(1)}, u32[]{:S(2)}, u32[]{:S(2)}) async-start(bf16[16,72,128]{2,1,0:T(8,128)(2,1)} %shard_map.55), calls=%async_computation.3 | async-start | bytes 589824 | tf_op jit(solution)/shard_map/all_to_all | solution.py:195
  6.1 0.7 %copy-start.3 = (f32[128,8]{0,1:T(8,128)S(1)}, f32[128,8]{0,1:T(8,128)}, u32[]{:S(2)}) copy-start(f32[128,8]{0,1:T(8,128)} %param.14) | copy-start | bytes 12292
  13.8 0.7 %collective-permute-start = (bf16[64,128]{1,0:T(8,128)(2,1)S(1)}, bf16[64,128]{1,0:T(8,128)(2,1)S(1)}, u32[]{:S(2)}, u32[]{:S(2)}) collective-permute-start(bf16[64,128]{1,0:T(8,128)(2,1)S(1)} %shard_map.58), channel_id=1, source_target_pairs={{0,128},{64,192},{1,129},{65,193},{2,130},{66,194},{3,131},{67,195... | collective-permute-start | bytes 49160 | tf_op jit(solution)/shard_map/ppermute | solution.py:261
  14.5 17.1 %collective-permute-start.2 = (bf16[64,128]{1,0:T(8,128)(2,1)S(1)}, bf16[64,128]{1,0:T(8,128)(2,1)S(1)}, u32[]{:S(2)}, u32[]{:S(2)}) collective-permute-start(bf16[64,128]{1,0:T(8,128)(2,1)S(1)} %shard_map.59), channel_id=1, source_target_pairs={{192,384},{128,320},{193,385},{129,321},{194,386},{130,322},{195,3... | collective-permute-start | bytes 49160 | tf_op jit(solution)/shard_map/ppermute | solution.py:266
  15.8 15.8 %collective-permute-start.1 = (bf16[64,128]{1,0:T(8,128)(2,1)S(1)}, bf16[64,128]{1,0:T(8,128)(2,1)S(1)}, u32[]{:S(2)}, u32[]{:S(2)}) collective-permute-start(bf16[64,128]{1,0:T(8,128)(2,1)S(1)} %shard_map.59), channel_id=1, source_target_pairs={{192,256},{128,448},{193,257},{129,449},{194,258},{130,450},{195,2... | collective-permute-start | bytes 49160 | tf_op jit(solution)/shard_map/ppermute | solution.py:265
  31.7 10.0 %copy-start.4 = (f32[1024]{0:T(1024)S(1)}, f32[1024]{0:T(1024)}, u32[]{:S(2)}) copy-start(f32[1024]{0:T(1024)} %param.15) | copy-start | bytes 12292

commit v8 on v7

--- a/solution.py
+++ b/solution.py
@@ -202,9 +202,9 @@
     half = heads * HEAD_DIM // members
     mac = 2 * heads * tok * HEAD_DIM * HEAD_DIM
     assert groups == 8
-    pair, four = [1, 0], [1, 3, 2, 0]
-    order = rotated(members, (13 * members) // 16)
-    y_order = rotated(mps, mps // 2)
+    pair, four = [1, 0], [1, 0, 3, 2]
+    order = rotated(members, (5 * members) // 16)
+    y_order = [mps // 2, *(y for y in range(mps) if y != mps // 2)]
     gates = log_decay.T
     (own,) = local(
         states_kernel,

time: 52.3 us -> 51.8 us (level)
  the two profiles are of different devices: /device:TPU:422 before, /device:TPU:406 now
where the time goes in v8:
time: 51.8 us; the launch traced here: 51.4 us
  blocking collectives  31.3 us (60%)
  waiting for transfers between devices  7.42 us (14%)
  starting transfers between devices  6.35 us (12%)
  Pallas kernels  4.77 us (9%)
  other arithmetic  0.72 us (1%)
  local copies, waits for them, and re-layouts  0.7 us (1%)
    all_to_all x2, blocking collectives, exchange(): return lax.all_to_all(a, axis, 0, 0, tiled=True, axis_index_groups=[order])  20.1 us
    all_to_all x1, blocking collectives, among(): lax.all_to_all(a, 'zh', 0, 0, tiled=True, axis_index_groups=lists)  11.2 us
    all_to_all x1, waiting for transfers between devices, exchange(): return lax.all_to_all(a, axis, 0, 0, tiled=True, axis_index_groups=[order])  5.37 us
    pallas_call x7, Pallas kernels, local(): pl.pallas_call(kernel, out_shape=[jax.ShapeDtypeStruct(shape, dtype) for...  4.77 us
    all_to_all x1, starting transfers between devices, exchange(): return lax.all_to_all(a, axis, 0, 0, tiled=True, axis_index_groups=[order])  3.73 us
    ppermute x1, waiting for transfers between devices, body(): came_b = lax.ppermute(sum1, 'zh', [(3, 6), (2, 5)])  2.04 us
    ppermute x1, starting transfers between devices, body(): came_b = lax.ppermute(sum1, 'zh', [(3, 6), (2, 5)])  1.29 us
  transfers between devices with their start and end apart: 4, of which 2 were waited for; matrix products, arithmetic and copies ran while one was open for 0% of the time, Pallas kernels for 3%

profile of v8, /device:TPU:406, one launch (start us, length us, event | category | flops | bytes accessed | tf_op | source)
XLA Modules:
  0.0 51.4 jit_solution(3856191480755528629)
XLA Ops:
  0.0 0.0 copy-start.2
  0.0 2.4 %shard_map.55 = bf16[16,72,128]{2,1,0:T(8,128)(2,1)} custom-call(bf16[128,1024]{1,0:T(8,128)(2,1)} %k_ref.1, bf16[128,1024]{1,0:T(8,128)(2,1)} %v_ref.1, f32[8,128]{1,0:T(8,128)} %bitcast.13), custom_call_target="tpu_custom_call" | custom-call | flops 33554432 | bytes 528384 | tf_op jit(solution)/shard_map/pallas_call | solution.py:179
  2.4 0.0 copy-start
  2.4 0.0 copy-start.1
  2.4 3.7 %all-to-all-start.3 = ((bf16[16,72,128]{2,1,0:T(8,128)(2,1)}), bf16[16,72,128]{2,1,0:T(8,128)(2,1)S(1)}, u32[]{:S(2)}, u32[]{:S(2)}) async-start(bf16[16,72,128]{2,1,0:T(8,128)(2,1)} %shard_map.55), calls=%async_computation.3 | async-start | bytes 589824 | tf_op jit(solution)/shard_map/all_to_all | solution.py:195
  6.1 0.0 copy-start.3
  6.2 0.0 copy-done.2
  6.2 0.0 copy-done
  6.2 0.0 copy-done.1
  6.2 0.6 %copy-done.3 = f32[128,8]{0,1:T(8,128)S(1)} copy-done((f32[128,8]{0,1:T(8,128)S(1)}, f32[128,8]{0,1:T(8,128)}, u32[]{:S(2)}) %copy-start.3) | copy-done | bytes 4120
  6.8 1.4 %shard_map.56 = (f32[128,1024]{1,0:T(8,128)S(1)}, f32[128,8]{1,0:T(8,128)S(1)}) custom-call(bf16[128,1024]{1,0:T(8,128)(2,1)S(1)} %copy-done.2, bf16[128,1024]{1,0:T(8,128)(2,1)S(1)} %copy-done, bf16[128,1024]{1,0:T(8,128)(2,1)S(1)} %copy-done.1, f32[8,128]{1,0:T(8,128)S(1)} %bitcast.14), custom_call_target="tpu_custom_call" | custom-call | flops 67108864 | bytes 790528 | tf_op jit(solution)/shard_map/pallas_call | solution.py:179
  8.3 5.4 %all-to-all-done.3.x_ref = bf16[16,72,128]{2,1,0:T(8,128)(2,1)S(1)} async-done(((bf16[16,72,128]{2,1,0:T(8,128)(2,1)}), bf16[16,72,128]{2,1,0:T(8,128)(2,1)S(1)}, u32[]{:S(2)}, u32[]{:S(2)}) %all-to-all-start.3) | async-done | bytes 294944 | tf_op jit(solution)/shard_map/all_to_all | solution.py:195
  13.7 0.1 shard_map.57
  13.8 0.7 %collective-permute-start = (bf16[64,128]{1,0:T(8,128)(2,1)S(1)}, bf16[64,128]{1,0:T(8,128)(2,1)S(1)}, u32[]{:S(2)}, u32[]{:S(2)}) collective-permute-start(bf16[64,128]{1,0:T(8,128)(2,1)S(1)} %shard_map.58), channel_id=1, source_target_pairs={{0,128},{64,192},{1,129},{65,193},{2,130},{66,194},{3,131},{67,195... | collective-permute-start | bytes 49160 | tf_op jit(solution)/shard_map/ppermute | solution.py:261
  14.5 0.0 collective-permute-done.refs_0_.p1_ref
  14.5 1.3 %collective-permute-start.2 = (bf16[64,128]{1,0:T(8,128)(2,1)S(1)}, bf16[64,128]{1,0:T(8,128)(2,1)S(1)}, u32[]{:S(2)}, u32[]{:S(2)}) collective-permute-start(bf16[64,128]{1,0:T(8,128)(2,1)S(1)} %shard_map.59), channel_id=1, source_target_pairs={{192,384},{128,320},{193,385},{129,321},{194,386},{130,322},{195,3... | collective-permute-start | bytes 49160 | tf_op jit(solution)/shard_map/ppermute | solution.py:266
  15.8 0.7 %collective-permute-start.1 = (bf16[64,128]{1,0:T(8,128)(2,1)S(1)}, bf16[64,128]{1,0:T(8,128)(2,1)S(1)}, u32[]{:S(2)}, u32[]{:S(2)}) collective-permute-start(bf16[64,128]{1,0:T(8,128)(2,1)S(1)} %shard_map.59), channel_id=1, source_target_pairs={{192,256},{128,448},{193,257},{129,449},{194,258},{130,450},{195,2... | collective-permute-start | bytes 49160 | tf_op jit(solution)/shard_map/ppermute | solution.py:265
  16.5 11.2 %conditional.5 = (bf16[4,72,128]{2,1,0:T(8,128)(2,1)S(1)}) conditional(s32[]{:T(128)} %convert_element_type.11, bf16[4,72,128]{2,1,0:T(8,128)(2,1)S(1)} %get-tuple-element.36, bf16[4,72,128]{2,1,0:T(8,128)(2,1)S(1)} %get-tuple-element.36), branch_computations={%region_4.0_spmd, %region_5.0_spmd} | conditional | bytes 294920 | solution.py:268
  16.5 11.2 %all_to_all.29 = bf16[4,72,128]{2,1,0:T(8,128)(2,1)S(1)} all-to-all(bf16[4,72,128]{2,1,0:T(8,128)(2,1)S(1)} %copy.13), channel_id=1, replica_groups={{64,0,192,128},{320,256,448,384},{65,1,193,129},{321,257,449,385},{66,2..., dimensions={0} | all-to-all | bytes 147456 | tf_op jit(solution)/shard_map/cond/branch_1_fun/all_to_all | solution.py:251
  27.7 2.0 %collective-permute-done.2.pb_ref = bf16[64,128]{1,0:T(8,128)(2,1)S(1)} collective-permute-done((bf16[64,128]{1,0:T(8,128)(2,1)S(1)}, bf16[64,128]{1,0:T(8,128)(2,1)S(1)}, u32[]{:S(2)}, u32[]{:S(2)}) %collective-permute-start.2) | collective-permute-done | bytes 16416 | tf_op jit(solution)/shard_map/ppermute | solution.py:266
  29.8 0.0 collective-permute-done.1.pa_ref
  29.8 0.1 shard_map.60
  29.9 0.0 copy-start.4
  29.9 10.3 %all_to_all.30 = bf16[16,64,128]{2,1,0:T(8,128)(2,1)S(1)} all-to-all(bf16[16,64,128]{2,1,0:T(8,128)(2,1)S(1)} %shard_map.60), channel_id=1, replica_groups={{20,24,28,32,36,40,44,48,52,56,60,0,4,8,12,16},{21,25,29,33,37,41,45,49..., dimensions={0} | all-to-all | bytes 524288 | tf_op jit(solution)/shard_map/all_to_all | solution.py:195
  40.2 0.0 copy-done.4
  40.2 0.8 %shard_map.61 = bf16[4,32,1024]{2,1,0:T(8,128)(2,1)S(1)} custom-call(bf16[128,1024]{1,0:T(8,128)(2,1)S(1)} %copy-done.2, bf16[8,128,128]{2,1,0:T(8,128)(2,1)S(1)} %bitcast.12, f32[128,1024]{1,0:T(8,128)S(1)} %get-tuple-element.38.i_ref, f32[128,8]{1,0:T(8,128)S(1)} %get-tuple-element.39.e_ref, f32[1,1024]{1,0:T(1,128)S(1)} %bitcast.15), custom_call_target="tpu_custom_call" | custom-call | flops 33554432 | bytes 1056768 | tf_op jit(solution)/shard_map/pallas_call | solution.py:179
  40.9 9.8 %all_to_all.31 = bf16[4,32,1024]{2,1,0:T(8,128)(2,1)S(1)} all-to-all(bf16[4,32,1024]{2,1,0:T(8,128)(2,1)S(1)} %shard_map.61), channel_id=1, replica_groups={{2,0,1,3},{6,4,5,7},{10,8,9,11},{14,12,13,15},{18,16,17,19},{22,20,21,2..., dimensions={0} | all-to-all | bytes 524288 | tf_op jit(solution)/shard_map/all_to_all | solution.py:195
  50.7 0.7 %pad_maximum_fusion = bf16[32,4096]{1,0:T(8,128)(2,1)} fusion(bf16[32,1024]{1,0:T(8,128)(2,1)S(1)} %get-tuple-element.41, bf16[32,1024]{1,0:T(8,128)(2,1)S(1)} %get-tuple-element.42, bf16[32,1024]{1,0:T(8,128)(2,1)S(1)} %get-tuple-element.43, bf16[32,1024]{1,0:T(8,128)(2,1)S(1)} %get-tuple-element.40), kind=kLoop, calls=%fused_computation | loop fusion | flops 1048576 | bytes 524288 | tf_op jit(solution)/shard_map/concatenate | solution.py:295
  (7 shorter events, 0.1 us)
Async XLA Ops:
  0.0 6.2 %copy-start.2 = (bf16[128,1024]{1,0:T(8,128)(2,1)S(1)}, bf16[128,1024]{1,0:T(8,128)(2,1)}, u32[]{:S(2)}) copy-start(bf16[128,1024]{1,0:T(8,128)(2,1)} %q_ref.3) | copy-start | bytes 786436
  2.4 3.8 %copy-start = (bf16[128,1024]{1,0:T(8,128)(2,1)S(1)}, bf16[128,1024]{1,0:T(8,128)(2,1)}, u32[]{:S(2)}) copy-start(bf16[128,1024]{1,0:T(8,128)(2,1)} %k_ref.1) | copy-start | bytes 786436
  2.4 3.8 %copy-start.1 = (bf16[128,1024]{1,0:T(8,128)(2,1)S(1)}, bf16[128,1024]{1,0:T(8,128)(2,1)}, u32[]{:S(2)}) copy-start(bf16[128,1024]{1,0:T(8,128)(2,1)} %v_ref.1) | copy-start | bytes 786436
  2.4 11.2 %all-to-all-start.3 = ((bf16[16,72,128]{2,1,0:T(8,128)(2,1)}), bf16[16,72,128]{2,1,0:T(8,128)(2,1)S(1)}, u32[]{:S(2)}, u32[]{:S(2)}) async-start(bf16[16,72,128]{2,1,0:T(8,128)(2,1)} %shard_map.55), calls=%async_computation.3 | async-start | bytes 589824 | tf_op jit(solution)/shard_map/all_to_all | solution.py:195
  6.1 0.7 %copy-start.3 = (f32[128,8]{0,1:T(8,128)S(1)}, f32[128,8]{0,1:T(8,128)}, u32[]{:S(2)}) copy-start(f32[128,8]{0,1:T(8,128)} %param.14) | copy-start | bytes 12292
  13.8 0.7 %collective-permute-start = (bf16[64,128]{1,0:T(8,128)(2,1)S(1)}, bf16[64,128]{1,0:T(8,128)(2,1)S(1)}, u32[]{:S(2)}, u32[]{:S(2)}) collective-permute-start(bf16[64,128]{1,0:T(8,128)(2,1)S(1)} %shard_map.58), channel_id=1, source_target_pairs={{0,128},{64,192},{1,129},{65,193},{2,130},{66,194},{3,131},{67,195... | collective-permute-start | bytes 49160 | tf_op jit(solution)/shard_map/ppermute | solution.py:261
  14.5 15.2 %collective-permute-start.2 = (bf16[64,128]{1,0:T(8,128)(2,1)S(1)}, bf16[64,128]{1,0:T(8,128)(2,1)S(1)}, u32[]{:S(2)}, u32[]{:S(2)}) collective-permute-start(bf16[64,128]{1,0:T(8,128)(2,1)S(1)} %shard_map.59), channel_id=1, source_target_pairs={{192,384},{128,320},{193,385},{129,321},{194,386},{130,322},{195,3... | collective-permute-start | bytes 49160 | tf_op jit(solution)/shard_map/ppermute | solution.py:266
  15.8 13.9 %collective-permute-start.1 = (bf16[64,128]{1,0:T(8,128)(2,1)S(1)}, bf16[64,128]{1,0:T(8,128)(2,1)S(1)}, u32[]{:S(2)}, u32[]{:S(2)}) collective-permute-start(bf16[64,128]{1,0:T(8,128)(2,1)S(1)} %shard_map.59), channel_id=1, source_target_pairs={{192,256},{128,448},{193,257},{129,449},{194,258},{130,450},{195,2... | collective-permute-start | bytes 49160 | tf_op jit(solution)/shard_map/ppermute | solution.py:265
  29.9 10.3 %copy-start.4 = (f32[1024]{0:T(1024)S(1)}, f32[1024]{0:T(1024)}, u32[]{:S(2)}) copy-start(f32[1024]{0:T(1024)} %param.15) | copy-start | bytes 12292
